TPU v7x, 32 devices: a whole 2x2x4 slice. The times are simulated.
32 devices in a mesh: col: 4 (over z), grp: 8 (over y, x, core).
Axes of the slice: x: 2, y: 2, z: 4, core: 2. Of those that a mesh axis runs over, the one named last changes fastest.
Arguments:
- factor_rows: float32 [1024, 8, 4, 512], P('grp', None, 'col'), may hold values from -3 to 3, as said below
- new_rows: float32 [4096, 8, 4, 512], P('grp', None, 'col'), may hold values from -0.5 to 0.5
Outputs:
- updated_rows: float32 [1024, 8, 4, 512], P('grp', None, 'col')
Inputs may be any that keep to these rules, and one draw needn't show every extreme that they name: factor_rows is upper triangular in the global row and column numbers, with diagonal entries between 1 and 3.
All inputs are finite; a program needn't handle non-finite values.
Results may differ from a plain program's by a relative error of at most 0.00008.
Values sent between devices are 32-bit elements; how exact they have to be, the bound alone decides.
A program may use at most 128 MiB of HBM per device.

v0:
```python
import jax
import jax.numpy as jnp
from jax import lax
from jax.sharding import PartitionSpec as P


def from_root(value, axis, source):
    kept = jnp.where(lax.axis_index(axis) == source, value, 0).astype(value.dtype)
    return lax.psum(kept, axis)


def solve_lower(lower, right):
    return lax.linalg.triangular_solve(lower, right, left_side=True, lower=True)


def shards(factor_rows, new_rows):
    highest = lax.Precision.HIGHEST
    own_rows = factor_rows.shape[0]
    npanel = factor_rows.shape[1]
    width = factor_rows.shape[3]
    local = jnp.concatenate([factor_rows, new_rows], 0).reshape(-1, npanel * width)
    panel = local[:, :width]
    first = from_root(panel, "col", 0)
    second = from_root(panel, "col", 1)
    part_one = jnp.dot(first.T, local, precision=highest, preferred_element_type=jnp.float32)
    part_two = jnp.dot(second.T, local, precision=highest, preferred_element_type=jnp.float32)
    both = jnp.concatenate([first, second], 1)
    small_one = jnp.dot(first.T, both, precision=highest, preferred_element_type=jnp.float32)
    small_two = jnp.dot(second.T, second, precision=highest, preferred_element_type=jnp.float32)
    gram_one, gram_two, corner_one, corner_two = lax.psum(
        (part_one, part_two, small_one, small_two), "grp"
    )
    lower_one = jnp.linalg.cholesky(corner_one[:, :width])
    cross = solve_lower(lower_one, corner_one[:, width:])
    lower_two = jnp.linalg.cholesky(corner_two - jnp.dot(cross.T, cross, precision=highest))
    upper_one = solve_lower(lower_one, gram_one)
    upper_two = solve_lower(lower_two, gram_two - jnp.dot(cross.T, upper_one, precision=highest))
    stacked = jnp.concatenate([upper_one, upper_two], 0)
    mine = lax.dynamic_slice_in_dim(stacked, lax.axis_index("grp") * own_rows, own_rows, 0)
    return mine.reshape(own_rows, npanel, 1, width)


def solution(mesh):
    placed = (P("grp", None, "col", None), P("grp", None, "col", None))
    return jax.shard_map(
        shards, mesh=mesh, in_specs=placed, out_specs=P("grp", None, "col", None), check_vma=False
    )
```

profile of v0, /device:TPU:0, one launch (start us, length us, event | category | flops | bytes accessed | tf_op | source)
XLA Modules:
  0.0 875.4 jit_solution(3415831424378312356)
XLA Ops:
  6.5 59.2 %maximum_reduce_fusion = f32[640,8,512]{2,1,0:T(8,128)} fusion(f32[512,8,1,512]{3,2,1,0:T(1,128)} %param.6, f32[128,8,1,512]{3,2,1,0:T(1,128)} %param.5), kind=kLoop, calls=%fused_computation.12 | loop fusion | flops 2621440 | bytes 20971520 | tf_op jit(solution)/shard_map/concatenate | solution.py:21
  65.7 18.2 %copy.11 = f32[80,8,8,512]{3,1,2,0:T(8,128)} copy(f32[80,8,8,512]{3,2,1,0:T(8,128)} %bitcast.125) | data formatting | bytes 20971520
  83.9 3.2 slice_select_fusion
  87.2 107.3 %all-reduce.8.cloned.1.call-done = (f32[640,512]{1,0:T(8,128)}, f32[640,512]{1,0:T(8,128)}) async-done(((f32[640,512]{1,0:T(8,128)}, f32[640,512]{1,0:T(8,128)}), (f32[640,512]{1,0:T(8,128)}, f32[640,512]{1,0:T(8,128)})) %all-reduce.8.cloned.1.call-update) | async-done | bytes 2621456 | tf_op jit(solution)/shard_map/psum | solution.py:9
  194.5 24.5 %fusion.115 = f32[512,4096]{1,0:T(8,128)} fusion(f32[640,512]{1,0:T(8,128)} %get-tuple-element.52, f32[640,4096]{1,0:T(8,128)} %bitcast.121), kind=kOutput, calls=%fused_computation.189 | convolution fusion | flops 16106127360 | bytes 20185088 | tf_op jit(solution)/shard_map/dot_general | solution.py:26
  219.1 6.5 fusion.35
  225.6 23.1 %fusion.113 = f32[512,4096]{1,0:T(8,128)} fusion(f32[640,512]{1,0:T(8,128)S(1)} %copy-done.2, f32[640,4096]{1,0:T(8,128)S(1)} %bitcast.124), kind=kOutput, calls=%fused_computation.187 | convolution fusion | flops 16106127360 | bytes 20185088 | tf_op jit(solution)/shard_map/dot_general | solution.py:25
  248.7 3.8 fusion.114
  252.5 252.6 %all-reduce.6.cloned.1.call-done = (f32[512,4096]{1,0:T(8,128)}, f32[512,1024]{0,1:T(8,128)}, f32[512,4096]{1,0:T(8,128)}, f32[512,512]{0,1:T(8,128)}) async-done(((f32[512,4096]{1,0:T(8,128)}, f32[512,1024]{0,1:T(8,128)}, f32[512,4096]{1,0:T(8,128)}, f32[512,512]{0,1:T(8,128)}), (f32[512,4096]{1,0:T(8,128)}, f32[512,1024]{0,1:T(8,128)}, f32[512,4096]{1,0:T(8,128)}, ...) | async-done | bytes 19922960 | tf_op jit(solution)/shard_map/psum | solution.py:30
  505.2 2.4 slice.184
  507.6 1.6 copy.4
  510.4 11.7 %cholesky.286 = f32[128,128]{1,0:T(8,128)S(1)} custom-call(f32[128,128]{1,0:T(8,128)S(1)} %cholesky.426), custom_call_target="Cholesky" | custom-call | tf_op jit(solution)/shard_map/jit(cholesky)/cholesky | solution.py:33
  522.2 9.8 %custom-call.31 = f32[1,128,128]{1,2,0:T(8,128)S(1)} custom-call(f32[1,128,128]{2,1,0:T(8,128)S(1)} %get-tuple-element.78), custom_call_target="InvertDiagBlocksLowerTriangular" | custom-call | tf_op jit(solution)/shard_map/jit(cholesky)/cholesky | solution.py:33
  532.1 1.2 constant_dynamic-update-slice_fusion.1
  533.3 1.3 convolution_subtract_fusion.9
  534.6 12.1 %cholesky.305 = f32[128,128]{1,0:T(8,128)S(1)} custom-call(f32[128,128]{1,0:T(8,128)S(1)} %cholesky.430), custom_call_target="Cholesky" | custom-call | tf_op jit(solution)/shard_map/jit(cholesky)/cholesky | solution.py:33
  546.7 9.8 %custom-call.32 = f32[1,128,128]{1,2,0:T(8,128)S(1)} custom-call(f32[1,128,128]{2,1,0:T(8,128)S(1)} %get-tuple-element.75), custom_call_target="InvertDiagBlocksLowerTriangular" | custom-call | tf_op jit(solution)/shard_map/jit(cholesky)/cholesky | solution.py:33
  556.8 1.3 convolution_subtract_fusion.11
  558.1 11.7 %cholesky.326 = f32[128,128]{1,0:T(8,128)S(1)} custom-call(f32[128,128]{1,0:T(8,128)S(1)} %cholesky.435), custom_call_target="Cholesky" | custom-call | tf_op jit(solution)/shard_map/jit(cholesky)/cholesky | solution.py:33
  570.5 9.8 %custom-call.33 = f32[1,128,128]{1,2,0:T(8,128)S(1)} custom-call(f32[1,128,128]{2,1,0:T(8,128)S(1)} %get-tuple-element.72), custom_call_target="InvertDiagBlocksLowerTriangular" | custom-call | tf_op jit(solution)/shard_map/jit(cholesky)/cholesky | solution.py:33
  581.8 11.9 %cholesky.343 = f32[128,128]{1,0:T(8,128)S(1)} custom-call(f32[128,128]{1,0:T(8,128)S(1)} %convolution_subtract_fusion.13), custom_call_target="Cholesky" | custom-call | tf_op jit(solution)/shard_map/jit(cholesky)/cholesky | solution.py:33
  598.6 11.3 %while.5 = (s32[]{:T(128)}, f32[512,512]{1,0:T(8,128)}, s32[4,2]{0,1:T(2,128)S(1)}, f32[4,128,128]{2,1,0:T(8,128)S(1)}, s32[]{:T(128)}) while((s32[]{:T(128)}, f32[512,512]{1,0:T(8,128)}, s32[4,2]{0,1:T(2,128)S(1)}, f32[4,128,128]{2,1,0:T(8,128)S(1)}, s32[]{:T(128)}) %tuple.55), condition=%wide.while_cond, body=%wide.while_body.sunk | while | flops 2 | bytes 131181 | solution.py:13
  599.2 2.2 bitcast_dynamic-update-slice_fusion.4
  602.1 2.2 bitcast_dynamic-update-slice_fusion.4
  604.9 2.2 bitcast_dynamic-update-slice_fusion.4
  607.8 2.1 bitcast_dynamic-update-slice_fusion.4
  609.9 39.3 %custom-call.34 = f32[4,128,128]{1,2,0:T(8,128)S(1)} custom-call(f32[4,128,128]{2,1,0:T(8,128)S(1)} %get-tuple-element.29), custom_call_target="InvertDiagBlocksLowerTriangular" | custom-call | tf_op jit(solution)/shard_map/triangular_solve/custom-call.3 | solution.py:13
  649.7 1.4 convolution_subtract_fusion.6
  651.6 2.0 convolution_subtract_fusion.5
  654.0 2.5 convolution_subtract_fusion.7
  657.0 1.9 convolution_subtract_fusion.4
  660.5 11.7 %cholesky.358 = f32[128,128]{1,0:T(8,128)S(1)} custom-call(f32[128,128]{1,0:T(8,128)S(1)} %cholesky.439), custom_call_target="Cholesky" | custom-call | tf_op jit(solution)/shard_map/jit(cholesky)/cholesky | solution.py:35
  672.3 10.2 %custom-call.35 = f32[1,128,128]{1,2,0:T(8,128)S(1)} custom-call(f32[1,128,128]{2,1,0:T(8,128)S(1)} %get-tuple-element.68), custom_call_target="InvertDiagBlocksLowerTriangular" | custom-call | tf_op jit(solution)/shard_map/jit(cholesky)/cholesky | solution.py:35
  682.5 1.2 constant_dynamic-update-slice_fusion
  683.8 1.3 convolution_subtract_fusion.8
  685.0 11.7 %cholesky.377 = f32[128,128]{1,0:T(8,128)S(1)} custom-call(f32[128,128]{1,0:T(8,128)S(1)} %cholesky.443), custom_call_target="Cholesky" | custom-call | tf_op jit(solution)/shard_map/jit(cholesky)/cholesky | solution.py:35
  698.1 9.8 %custom-call.36 = f32[1,128,128]{1,2,0:T(8,128)S(1)} custom-call(f32[1,128,128]{2,1,0:T(8,128)S(1)} %get-tuple-element.65), custom_call_target="InvertDiagBlocksLowerTriangular" | custom-call | tf_op jit(solution)/shard_map/jit(cholesky)/cholesky | solution.py:35
  708.2 1.3 convolution_subtract_fusion.10
  709.5 11.7 %cholesky.398 = f32[128,128]{1,0:T(8,128)S(1)} custom-call(f32[128,128]{1,0:T(8,128)S(1)} %cholesky.448), custom_call_target="Cholesky" | custom-call | tf_op jit(solution)/shard_map/jit(cholesky)/cholesky | solution.py:35
  722.0 10.0 %custom-call.37 = f32[1,128,128]{1,2,0:T(8,128)S(1)} custom-call(f32[1,128,128]{2,1,0:T(8,128)S(1)} %get-tuple-element.62), custom_call_target="InvertDiagBlocksLowerTriangular" | custom-call | tf_op jit(solution)/shard_map/jit(cholesky)/cholesky | solution.py:35
  733.4 11.7 %cholesky.415 = f32[128,128]{1,0:T(8,128)S(1)} custom-call(f32[128,128]{1,0:T(8,128)S(1)} %convolution_subtract_fusion.12), custom_call_target="Cholesky" | custom-call | tf_op jit(solution)/shard_map/jit(cholesky)/cholesky | solution.py:35
  748.4 8.1 while.6
  749.0 1.3 bitcast_dynamic-update-slice_fusion.5
  751.1 1.3 bitcast_dynamic-update-slice_fusion.5
  753.1 1.3 bitcast_dynamic-update-slice_fusion.5
  755.1 1.3 bitcast_dynamic-update-slice_fusion.5
  756.5 40.1 %custom-call.38 = f32[4,128,128]{1,2,0:T(8,128)} custom-call(f32[4,128,128]{2,1,0:T(8,128)S(1)} %get-tuple-element.30), custom_call_target="InvertDiagBlocksLowerTriangular" | custom-call | tf_op jit(solution)/shard_map/triangular_solve/custom-call.3 | solution.py:13
  796.6 3.5 fusion.48
  800.1 3.6 convolution_subtract_fusion.3
  803.7 1.9 fusion.95
  805.7 4.1 convolution_subtract_fusion.2
  809.8 1.9 fusion.97
  811.7 6.1 fusion.26
  817.8 1.9 fusion.99
  819.7 17.2 %fusion.8 = f32[512,4096]{1,0:T(8,128)} fusion(f32[512,4096]{1,0:T(8,128)} %get-tuple-element.49, f32[128,4096]{1,0:T(8,128)S(1)} %fusion.99, f32[128,4096]{1,0:T(8,128)S(1)} %fusion.97, f32[128,4096]{1,0:T(8,128)S(1)} %fusion.95, f32[128,4096]{1,0:T(8,128)S(1)} %fusion.48, f32[128,512]{1,0:T(8,128)S(1)} %fusion.98, f32[128,512]{1,0:T(8,128)S(1)} %fusion.96, ...), kind=kOutput, calls=%fused_computation.21 | convolution fusion | flops 12894076928 | bytes 26214400 | tf_op jit(solution)/shard_map/dot_general | solution.py:37
  836.9 3.5 fusion.46
  840.4 3.7 convolution_subtract_fusion.1
  844.2 1.9 fusion.83
  846.2 3.2 convolution_subtract_fusion
  849.4 2.0 fusion.81
  851.4 5.1 fusion.23
  856.4 3.3 fusion.80
  859.7 3.9 fusion.42
  863.6 4.7 reshape.50
  (87 shorter events, 19.6 us)
Async XLA Ops:
  6.5 188.0 %all-reduce.8.cloned.1.call-start = ((), (), s32[]{:S(2)}) async-start(), calls=%async_computation.1 | async-start | bytes 5242880 | tf_op jit(solution)/shard_map/psum | solution.py:9
  87.1 138.4 %slice-start = ((s8[10485760]{0:T(1024)(128)(4,1)}), s8[2097152]{0:T(1024)(128)(4,1)S(1)}, s32[]{:S(2)}) async-start(s8[10485760]{0:T(1024)(128)(4,1)} %bitcast.122), calls=%async_computation.2 | async-start | bytes 4194304
  87.2 418.0 %all-reduce.6.cloned.1.call-start = ((), (), s32[]{:S(2)}) async-start(), calls=%async_computation | async-start | bytes 39845888 | tf_op jit(solution)/shard_map/psum | solution.py:30
  194.5 24.6 %copy-start.1 = (f32[640,512]{1,0:T(8,128)S(1)}, f32[640,512]{1,0:T(8,128)}, u32[]{:S(2)}) copy-start(f32[640,512]{1,0:T(8,128)} %get-tuple-element.52) | copy-start | bytes 3932164
  194.5 24.6 %copy-start.2 = (f32[640,512]{1,0:T(8,128)S(1)}, f32[640,512]{1,0:T(8,128)}, u32[]{:S(2)}) copy-start(f32[640,512]{1,0:T(8,128)} %get-tuple-element.51) | copy-start | bytes 3932164
  194.5 31.1 %slice-start.1 = ((s8[10485760]{0:T(1024)(128)(4,1)}), s8[4194304]{0:T(1024)(128)(4,1)S(1)}, s32[]{:S(2)}) async-start(s8[10485760]{0:T(1024)(128)(4,1)} %bitcast.122), calls=%async_computation.3 | async-start | bytes 8388608
  194.5 31.1 %slice-start.2 = ((s8[10485760]{0:T(1024)(128)(4,1)}), s8[4194304]{0:T(1024)(128)(4,1)S(1)}, s32[]{:S(2)}) async-start(s8[10485760]{0:T(1024)(128)(4,1)} %bitcast.122), calls=%async_computation.4 | async-start | bytes 8388608
  505.2 4.0 copy-start.3
  509.4 1.0 copy-start.6
  651.2 5.8 copy-start.7
  659.4 1.0 copy-start.5
  756.5 43.6 %copy-start.4 = (f32[512,512]{1,0:T(8,128)}, f32[512,512]{1,0:T(8,128)S(1)}, u32[]{:S(2)}) copy-start(f32[512,512]{1,0:T(8,128)S(1)} %get-tuple-element.201) | copy-start | bytes 3145732
  819.7 17.2 %copy-start.8 = (f32[4,128,128]{1,2,0:T(8,128)S(1)}, f32[4,128,128]{1,2,0:T(8,128)}, u32[]{:S(2)}) copy-start(f32[4,128,128]{1,2,0:T(8,128)} %custom-call.38) | copy-start | bytes 786436
  840.4 5.7 copy-start
Sparse Core Ops, SparseCore 0:
  87.3 107.1 all-reduce.7
  252.6 252.4 all-reduce.5
where the time goes:
time: 880 us; the launch traced here: 875 us
  waiting for transfers between devices  360 us (41%)
  other arithmetic  306 us (35%)
  matrix products  141 us (16%)
  local copies, waits for them, and re-layouts  48.8 us (6%)
  between operations  19.1 us (2%)
    psum x1, waiting for transfers between devices, shards(): lax.psum((part_one, part_two, small_one, small_two), 'grp')  253 us
    psum x1, waiting for transfers between devices, from_root(): return lax.psum(kept, axis)  107 us
    another operation x5, other arithmetic, solve_lower(): return lax.linalg.triangular_solve(lower, right, left_side=True, lower=True)  80.7 us
    another operation x15, other arithmetic, shards(): jnp.linalg.cholesky(corner_two - jnp.dot(cross.T, cross, precision=highest))  79.6 us
    another operation x14, other arithmetic, shards(): lower_one = jnp.linalg.cholesky(corner_one[:, :width])  79 us
    concatenate x1, other arithmetic, shards(): jnp.concatenate([factor_rows, new_rows], 0).reshape(-1, npanel * width)  59.2 us
    another operation x21, matrix products, solve_lower(): return lax.linalg.triangular_solve(lower, right, left_side=True, lower=True)  53.4 us
    dot_general x1, matrix products, shards(): jnp.dot(second.T, local, precision=highest, preferred_element_type=jnp.fl...  24.5 us
  transfers between devices with their start and end apart: 2, of which 2 were waited for; matrix products, arithmetic and copies ran while one was open for 0% of the time, Pallas kernels for 0%

commit v1 on v0

v1 whole, which is shorter than its diff:
```python
import jax
import jax.numpy as jnp
from jax import lax
from jax.experimental import pallas as pl
from jax.experimental.pallas import tpu as pltpu
from jax.sharding import PartitionSpec as P

TILE = 128
SLAB = 8


def inverse_factor_tile(d):
    count = TILE // SLAB
    rows = [d[SLAB * q:SLAB * (q + 1), :] for q in range(count)]
    sub = lax.broadcasted_iota(jnp.int32, (SLAB, TILE), 0)
    lane = lax.broadcasted_iota(jnp.int32, (SLAB, TILE), 1)
    full = (SLAB, TILE)
    for q in range(count):
        at = SLAB * q
        inside = (lane >= at) & (lane < at + SLAB)
        slab = rows[q]
        cols = [jnp.broadcast_to(slab[:, at + j:at + j + 1], full) for j in range(SLAB)]
        t = jnp.where(inside, jnp.where(lane - at == sub, 1.0, 0.0), slab)
        pivots = jnp.ones(full, jnp.float32)
        for j in range(SLAB):
            p = jnp.broadcast_to(cols[j][j:j + 1, :], full)
            pivots = jnp.where(sub == j, p, pivots)
            if j == SLAB - 1:
                break
            m = jnp.where(sub > j, cols[j] * (1.0 / p), 0.0)
            for k in range(j + 1, SLAB):
                cols[k] = cols[k] - m * jnp.broadcast_to(cols[k][j:j + 1, :], full)
            t = t - m * jnp.broadcast_to(t[j:j + 1, :], full)
        y = lax.rsqrt(pivots)
        y = y * (1.5 - 0.5 * pivots * y * y)
        t = t * y
        rows[q] = t
        if q + 1 < count:
            turned = t.T
            lines = [jnp.broadcast_to(t[j:j + 1, :], full) for j in range(SLAB)]
            for i in range(q + 1, count):
                left = turned[SLAB * i:SLAB * (i + 1), :]
                total = jnp.where(inside, 0.0, rows[i])
                for j in range(SLAB):
                    total = total - jnp.broadcast_to(left[:, j:j + 1], full) * lines[j]
                rows[i] = total
    done = jnp.concatenate(rows, 0)
    r = lax.broadcasted_iota(jnp.int32, (TILE, TILE), 0)
    c = lax.broadcasted_iota(jnp.int32, (TILE, TILE), 1)
    return jnp.where(r >= c, done, 0.0)


def inverse_factor_kernel(s_ref, m_ref):
    n = s_ref.shape[0]
    count = n // TILE
    highest = lax.Precision.HIGHEST
    m_ref[...] = s_ref[...]
    r = lax.broadcasted_iota(jnp.int32, (TILE, TILE), 0)
    c = lax.broadcasted_iota(jnp.int32, (TILE, TILE), 1)
    eye = jnp.where(r == c, 1.0, 0.0).astype(jnp.float32)

    @pl.loop(0, count)
    def _(k):
        here = pl.ds(pl.multiple_of(k * TILE, TILE), TILE)
        inverse = inverse_factor_tile(m_ref[here, here])
        m_ref[here, here] = eye
        line = jnp.dot(inverse, m_ref[here, :], precision=highest, preferred_element_type=jnp.float32)
        m_ref[here, :] = line

        @pl.loop(k + 1, count)
        def _(i):
            there = pl.ds(pl.multiple_of(i * TILE, TILE), TILE)
            m_ref[there, here] = jnp.zeros((TILE, TILE), jnp.float32)
            m_ref[there, :] -= lax.dot_general(
                m_ref[here, there], m_ref[here, :], (((0,), (0,)), ((), ())),
                precision=highest, preferred_element_type=jnp.float32,
            )

    @pl.loop(0, count)
    def _(k):
        here = pl.ds(pl.multiple_of(k * TILE, TILE), TILE)
        row = lax.broadcasted_iota(jnp.int32, (TILE, n), 0) + k * TILE
        col = lax.broadcasted_iota(jnp.int32, (TILE, n), 1)
        m_ref[here, :] = jnp.where(row >= col, m_ref[here, :], 0.0)


def inverse_factor(s):
    n = s.shape[0]
    return pl.pallas_call(
        inverse_factor_kernel,
        out_shape=jax.ShapeDtypeStruct((n, n), jnp.float32),
        in_specs=[pl.BlockSpec(memory_space=pltpu.VMEM)],
        out_specs=pl.BlockSpec(memory_space=pltpu.VMEM),
        compiler_params=pltpu.CompilerParams(vmem_limit_bytes=24 * 2**20),
        cost_estimate=pl.CostEstimate(flops=60 * 10**9, bytes_accessed=8 * 2**20, transcendentals=0),
    )(s)


def leading_panels(panel, ncol):
    me = lax.axis_index("col")
    back = lax.ppermute(panel, "col", [(1, 0)])
    first = panel
    second = jnp.where(me == 0, back, panel)
    sent = panel
    for t in range(ncol - 1):
        pairs = [(t, t + 1)] + ([(t + 1, t + 2)] if t + 2 < ncol else [])
        sent = lax.ppermute(sent, "col", pairs)
        first = jnp.where(me == t + 1, sent, first)
        if t + 2 < ncol:
            second = jnp.where(me == t + 2, sent, second)
    return first, second


def make_shards(ncol, ngrp):
    def shards(factor_rows, new_rows):
        high, highest = lax.Precision.HIGH, lax.Precision.HIGHEST
        own_rows = factor_rows.shape[0]
        npanel = factor_rows.shape[1]
        width = factor_rows.shape[3]
        panels = [
            jnp.concatenate([factor_rows[:, p, 0, :], new_rows[:, p, 0, :]], 0)
            for p in range(npanel)
        ]
        total = panels[0].shape[0]
        cut = total // 2
        top = leading_panels(panels[0][:cut], ncol)
        low = leading_panels(panels[0][cut:], ncol)
        both = jnp.concatenate(
            [jnp.concatenate(top, 1), jnp.concatenate(low, 1)], 0
        )
        split = max(1, ngrp // npanel)
        piece = width // split
        turned = (((0,), (0,)), ((), ()))
        corner = lax.dot_general(both, both, turned, precision=highest, preferred_element_type=jnp.float32)
        corner = lax.psum(corner, "grp")
        parts = [
            lax.dot_general(
                both, x[:, q * piece:(q + 1) * piece], turned,
                precision=high, preferred_element_type=jnp.float32,
            )
            for x in panels for q in range(split)
        ]
        per = npanel * split // ngrp
        gram = jnp.stack(parts, 0)
        gram = lax.psum_scatter(gram, "grp", scatter_dimension=0, tiled=True)
        inverse = inverse_factor(corner)
        done = [
            jnp.dot(inverse, gram[p], precision=high, preferred_element_type=jnp.float32)
            for p in range(per)
        ]
        result = jnp.stack(done, 0).reshape(per, ngrp, own_rows, piece)
        result = lax.all_to_all(result, "grp", split_axis=1, concat_axis=0, tiled=True)
        result = result.reshape(npanel, split, own_rows, piece)
        return result.transpose(2, 0, 1, 3).reshape(own_rows, npanel, 1, width)

    return shards


def solution(mesh):
    placed = P("grp", None, "col", None)
    return jax.shard_map(
        make_shards(mesh.shape["col"], mesh.shape["grp"]),
        mesh=mesh, in_specs=(placed, placed), out_specs=placed, check_vma=False,
    )
```

time: 880 us -> 367 us (0.42)
  other arithmetic: 306 us -> 3.8 us
  waiting for transfers between devices: 360 us -> 144 us
  matrix products: 141 us -> 51.2 us
  Pallas kernels: 0 us -> 68.8 us
  blocking collectives: 0 us -> 29.1 us
  starting transfers between devices: 0.04 us -> 17 us
  local copies, waits for them, and re-layouts: 48.8 us -> 34.3 us
    psum x2 -> x1, waiting for transfers between devices: 360 us -> 70.2 us  [shards(): corner = lax.psum(corner, 'grp')]
    another operation x34 -> x0, other arithmetic: 239 us -> none  [the longest x5 80.7 us: solve_lower(): return lax.linalg.triangular_solve(lower, right, left_side=True, lower=True)]
    pallas_call x0 -> x1, Pallas kernels: none -> 68.8 us  [inverse_factor(): pl.pallas_call(inverse_factor_kernel, out_shape=jax.ShapeDtypeStruct((n,...]
    another operation x33 -> x0, matrix products: 64.3 us -> none  [the longest x21 53.4 us: solve_lower(): return lax.linalg.triangular_solve(lower, right, left_side=True, lower=True)]
    concatenate x2 -> x0, other arithmetic: 63.1 us -> none  [the longest x1 59.2 us: shards(): jnp.concatenate([factor_rows, new_rows], 0).reshape(-1, npanel * width)]
    reduce_scatter x0 -> x1, waiting for transfers between devices: none -> 47.2 us  [shards(): gram = lax.psum_scatter(gram, 'grp', scatter_dimension=0, tiled=True)]
    all_to_all x0 -> x1, blocking collectives: none -> 29.1 us  [shards(): lax.all_to_all(result, 'grp', split_axis=1, concat_axis=0, tiled=True)]
    ppermute x0 -> x8, waiting for transfers between devices: none -> 26.7 us  [the longest x6 17.2 us: leading_panels(): sent = lax.ppermute(sent, 'col', pairs)]
  transfers between devices with their start and end apart: 2 -> 10, of which waited for: 2 -> 6; matrix products, arithmetic and copies ran while one was open for 0% -> 12% of each run, Pallas kernels for 0% -> 19%
where the time goes in v1:
time: 367 us; the launch traced here: 363 us
  waiting for transfers between devices  144 us (39%)
  Pallas kernels  68.8 us (19%)
  matrix products  51.2 us (14%)
  local copies, waits for them, and re-layouts  34.3 us (9%)
  blocking collectives  29.1 us (8%)
  starting transfers between devices  17 us (5%)
  between operations  14.1 us (4%)
  other arithmetic  3.8 us (1%)
    psum x1, waiting for transfers between devices, shards(): corner = lax.psum(corner, 'grp')  70.2 us
    pallas_call x1, Pallas kernels, inverse_factor(): pl.pallas_call(inverse_factor_kernel, out_shape=jax.ShapeDtypeStruct((n,...  68.8 us
    reduce_scatter x1, waiting for transfers between devices, shards(): gram = lax.psum_scatter(gram, 'grp', scatter_dimension=0, tiled=True)  47.2 us
    dot_general x8, matrix products, shards(): lax.dot_general(both, x[:, q * piece:(q + 1) * piece], turned, precision=...  32.5 us
    all_to_all x1, blocking collectives, shards(): lax.all_to_all(result, 'grp', split_axis=1, concat_axis=0, tiled=True)  29.1 us
    ppermute x6, waiting for transfers between devices, leading_panels(): sent = lax.ppermute(sent, 'col', pairs)  17.2 us
    unnamed x70, local copies, waits for them, and re-layouts  16.2 us
    ppermute x6, starting transfers between devices, leading_panels(): sent = lax.ppermute(sent, 'col', pairs)  14.2 us
  transfers between devices with their start and end apart: 10, of which 6 were waited for; matrix products, arithmetic and copies ran while one was open for 12% of the time, Pallas kernels for 19%

profile of v1, /device:TPU:0, one launch (start us, length us, event | category | flops | bytes accessed | tf_op | source)
XLA Modules:
  0.0 362.6 jit_solution(8112249079763167571)
XLA Ops:
  6.5 9.3 %fusion.38 = (f32[512,1,1,512]{3,2,1,0:T(1,128)S(1)}, f32[512,1,1,512]{3,2,1,0:T(1,128)}, f32[512,1,1,512]{3,2,1,0:T(1,128)}, f32[512,1,1,512]{3,2,1,0:T(1,128)}...) fusion(f32[512,8,1,512]{3,2,1,0:T(1,128)} %param.3), kind=kLoop, calls=%fused_computation.67 | loop fusion | bytes 16777216 | tf_op jit(solution)/shard_map/slice | solution.py:121
  15.8 0.1 copy.62
  15.9 1.5 copy-done.9
  17.4 2.1 fusion.39
  19.5 0.0 copy-start.10
  19.6 0.6 copy-done.10
  20.2 5.8 %collective-permute-start = (f32[320,512]{1,0:T(8,128)S(1)}, f32[320,512]{1,0:T(8,128)}, u32[]{:S(2)}, u32[]{:S(2)}) collective-permute-start(f32[320,512]{1,0:T(8,128)S(1)} %pad_maximum_fusion), channel_id=1, source_target_pairs={{0,8},{8,16},{1,9},{9,17},{2,10},{10,18},{3,11},{11,19},{4,12},{12... | collective-permute-start | bytes 1966088 | tf_op jit(solution)/shard_map/ppermute | solution.py:107
  26.0 1.5 slice.61
  27.5 0.9 copy.64
  28.4 3.5 collective-permute-start.4
  31.9 8.3 %collective-permute-done = f32[320,512]{1,0:T(8,128)} collective-permute-done((f32[320,512]{1,0:T(8,128)S(1)}, f32[320,512]{1,0:T(8,128)}, u32[]{:S(2)}, u32[]{:S(2)}) %collective-permute-start) | collective-permute-done | bytes 655392 | tf_op jit(solution)/shard_map/ppermute | solution.py:107
  40.3 1.6 collective-permute-start.1
  41.8 1.3 collective-permute-start.3
  43.1 1.3 collective-permute-start.7
  44.4 8.9 %collective-permute-done.4 = f32[320,512]{1,0:T(8,128)} collective-permute-done((f32[320,512]{1,0:T(8,128)}, f32[320,512]{1,0:T(8,128)}, u32[]{:S(2)}, u32[]{:S(2)}) %collective-permute-start.4) | collective-permute-done | bytes 655392 | tf_op jit(solution)/shard_map/ppermute | solution.py:107
  53.3 1.5 collective-permute-start.5
  54.8 0.8 copy_bitcast_fusion.13
  55.6 1.0 copy.63
  56.7 1.1 copy.65
  57.8 0.0 copy-start.3
  57.8 0.8 copy_bitcast_fusion.11
  58.6 0.0 collective-permute-done.1
  58.6 0.7 collective-permute-start.2
  59.3 1.6 copy_bitcast_fusion.5
  60.9 0.0 collective-permute-done.5
  60.9 1.2 collective-permute-start.6
  62.2 1.5 copy_bitcast_fusion.3
  63.7 0.6 collective-permute-done.3
  64.3 0.0 collective-permute-done.2
  64.3 1.9 select_select_fusion.3
  66.1 8.9 %collective-permute-done.7 = f32[320,512]{1,0:T(8,128)} collective-permute-done((f32[320,512]{1,0:T(8,128)}, f32[320,512]{1,0:T(8,128)}, u32[]{:S(2)}, u32[]{:S(2)}) %collective-permute-start.7) | collective-permute-done | bytes 655392 | tf_op jit(solution)/shard_map/ppermute | solution.py:101
  75.1 0.0 collective-permute-done.6
  75.1 1.9 select_select_fusion.1
  77.0 0.8 copy-done.23
  77.8 0.2 copy-done.25
  78.0 12.7 %fusion.37 = f32[1024,1024]{1,0:T(8,128)} fusion(f32[320,512]{1,0:T(8,128)S(1)} %get-tuple-element.24, f32[320,512]{1,0:T(8,128)S(1)} %get-tuple-element.23, f32[320,512]{1,0:T(8,128)S(1)} %get-tuple-element.22, f32[320,512]{1,0:T(8,128)S(1)} %get-tuple-element.21), kind=kOutput, calls=%fused_computation.66 | convolution fusion | flops 8055029760 | bytes 6815744 | tf_op jit(solution)/shard_map/dot_general | solution.py:134
  90.8 0.0 all-reduce.2.cloned.1.call-update
  90.8 0.2 reduce-scatter.2.cloned.1.call-start
  91.0 0.7 copy-done.13
  91.7 0.1 copy-done.14
  91.8 0.3 copy-done.2
  92.1 0.2 copy_bitcast_fusion.1
  92.3 0.8 copy-done.8
  93.1 0.0 copy-done.11
  93.1 0.2 copy-done.22
  93.3 0.2 copy-done.24
  93.5 0.2 copy-done.26
  93.7 4.0 %bitcast_dynamic-update-slice_fusion.7 = f32[8,1024,512]{2,1,0:T(8,128)} fusion(f32[512,512]{1,0:T(8,128)S(1)} %bitcast.77, f32[128,512]{1,0:T(8,128)S(1)} %bitcast.79, f32[320,512]{1,0:T(8,128)S(1)} %copy-done.26, f32[320,512]{1,0:T(8,128)S(1)} %copy-done.24, f32[320,512]{1,0:T(8,128)S(1)} %copy-done.22, f32[320,512]{1,0:T(8,128)S(1)} %get-tuple-element.21), kind=kOutput, calls=%fused_computation.10 | convolution fusion | flops 2015559680 | bytes 6029312 | tf_op jit(solution)/shard_map/dot_general | solution.py:137
  97.8 4.0 %bitcast_dynamic-update-slice_fusion.6 = f32[8,1024,512]{2,1,0:T(8,128)} fusion(f32[8,1024,512]{2,1,0:T(8,128)} %bitcast_dynamic-update-slice_fusion.7, f32[512,512]{1,0:T(8,128)S(1)} %bitcast.80, f32[128,512]{1,0:T(8,128)S(1)} %bitcast.81, f32[320,512]{1,0:T(8,128)S(1)} %copy-done.26, f32[320,512]{1,0:T(8,128)S(1)} %copy-done.24, ...), kind=kOutput, calls=%fused_computation.9 | convolution fusion | flops 2015559680 | bytes 6029312 | tf_op jit(solution)/shard_map/dot_general | solution.py:137
  101.8 4.1 %bitcast_dynamic-update-slice_fusion.5 = f32[8,1024,512]{2,1,0:T(8,128)} fusion(f32[8,1024,512]{2,1,0:T(8,128)} %bitcast_dynamic-update-slice_fusion.6, f32[512,512]{1,0:T(8,128)S(1)} %copy-done.19, f32[128,512]{1,0:T(8,128)S(1)} %copy-done.28, f32[320,512]{1,0:T(8,128)S(1)} %copy-done.26, f32[320,512]{1,0:T(8,128)S(1)} %copy-done.24, ...), kind=kOutput, calls=%fused_computation.8 | convolution fusion | flops 2015559680 | bytes 6029312 | tf_op jit(solution)/shard_map/dot_general | solution.py:137
  105.9 4.1 %bitcast_dynamic-update-slice_fusion.4 = f32[8,1024,512]{2,1,0:T(8,128)} fusion(f32[8,1024,512]{2,1,0:T(8,128)} %bitcast_dynamic-update-slice_fusion.5, f32[512,512]{1,0:T(8,128)S(1)} %copy-done.17, f32[128,512]{1,0:T(8,128)S(1)} %copy-done.27, f32[320,512]{1,0:T(8,128)S(1)} %copy-done.26, f32[320,512]{1,0:T(8,128)S(1)} %copy-done.24, ...), kind=kOutput, calls=%fused_computation.7 | convolution fusion | flops 2015559680 | bytes 6029312 | tf_op jit(solution)/shard_map/dot_general | solution.py:137
  110.0 4.3 %bitcast_dynamic-update-slice_fusion.3 = f32[8,1024,512]{2,1,0:T(8,128)} fusion(f32[8,1024,512]{2,1,0:T(8,128)} %bitcast_dynamic-update-slice_fusion.4, f32[512,512]{1,0:T(8,128)S(1)} %copy-done.20, f32[128,512]{1,0:T(8,128)S(1)} %copy-done.30, f32[320,512]{1,0:T(8,128)S(1)} %copy-done.26, f32[320,512]{1,0:T(8,128)S(1)} %copy-done.24, ...), kind=kOutput, calls=%fused_computation.6 | convolution fusion | flops 2015559680 | bytes 6029312 | tf_op jit(solution)/shard_map/dot_general | solution.py:137
  114.2 4.1 %bitcast_dynamic-update-slice_fusion.2 = f32[8,1024,512]{2,1,0:T(8,128)} fusion(f32[8,1024,512]{2,1,0:T(8,128)} %bitcast_dynamic-update-slice_fusion.3, f32[512,512]{1,0:T(8,128)S(1)} %copy-done.18, f32[128,512]{1,0:T(8,128)S(1)} %copy-done.29, f32[320,512]{1,0:T(8,128)S(1)} %copy-done.26, f32[320,512]{1,0:T(8,128)S(1)} %copy-done.24, ...), kind=kOutput, calls=%fused_computation.5 | convolution fusion | flops 2015559680 | bytes 6029312 | tf_op jit(solution)/shard_map/dot_general | solution.py:137
  118.3 4.0 %bitcast_dynamic-update-slice_fusion.1 = f32[8,1024,512]{2,1,0:T(8,128)} fusion(f32[8,1024,512]{2,1,0:T(8,128)} %bitcast_dynamic-update-slice_fusion.2, f32[512,512]{1,0:T(8,128)S(1)} %get-tuple-element.26, f32[128,512]{1,0:T(8,128)S(1)} %get-tuple-element.32, f32[320,512]{1,0:T(8,128)S(1)} %copy-done.26, f32[320,512]{1,0:T(8,128)S(1)} %copy-done.24, ...), kind=kOutput, calls=%fused_computation.4 | convolution fusion | flops 2015559680 | bytes 6029312 | tf_op jit(solution)/shard_map/dot_general | solution.py:137
  122.3 4.0 %bitcast_dynamic-update-slice_fusion = f32[8,1024,512]{2,1,0:T(8,128)} fusion(f32[8,1024,512]{2,1,0:T(8,128)} %bitcast_dynamic-update-slice_fusion.1, f32[512,512]{1,0:T(8,128)S(1)} %get-tuple-element.25, f32[128,512]{1,0:T(8,128)S(1)} %get-tuple-element.31, f32[320,512]{1,0:T(8,128)S(1)} %copy-done.26, f32[320,512]{1,0:T(8,128)S(1)} %copy-done.24, ...), kind=kOutput, calls=%fused_computation.3 | convolution fusion | flops 2015559680 | bytes 6029312 | tf_op jit(solution)/shard_map/dot_general | solution.py:137
  126.3 0.0 reduce-scatter.2.cloned.1.call-update
  126.4 70.2 %all-reduce.2.cloned.1.call-done.s_ref = f32[1024,1024]{1,0:T(8,128)} async-done(((f32[1024,1024]{1,0:T(8,128)}), f32[1024,1024]{1,0:T(8,128)}) %all-reduce.2.cloned.1.call-update) | async-done | bytes 4194320 | tf_op jit(solution)/shard_map/psum | solution.py:135
  196.6 2.2 copy-done.1
  198.8 68.8 %shard_map.28 = f32[1024,1024]{1,0:T(8,128)S(1)} custom-call(f32[1024,1024]{1,0:T(8,128)S(1)} %copy-done.1), custom_call_target="tpu_custom_call" | custom-call | flops 60000002048 | bytes 8388608 | tf_op jit(solution)/shard_map/pallas_call | solution.py:89
  267.6 2.0 copy-done
  269.5 47.2 %reduce-scatter.2.cloned.1.call-done = f32[1,1024,512]{2,1,0:T(8,128)} async-done(((f32[8,1024,512]{2,1,0:T(8,128)}), f32[1,1024,512]{2,1,0:T(8,128)}) %reduce-scatter.2.cloned.1.call-update) | async-done | bytes 2097168 | tf_op jit(solution)/shard_map/reduce_scatter | solution.py:145
  316.7 5.9 %fusion.2 = f32[1,8,128,512]{3,2,0,1:T(8,128)S(1)} fusion(f32[8,128,1024]{2,1,0:T(8,128)} %bitcast.74, f32[1,1024,512]{2,1,0:T(8,128)} %reduce-scatter.2.cloned.1.call-done), kind=kOutput, calls=%fused_computation.11 | convolution fusion | flops 3221225472 | bytes 8388608 | tf_op jit(solution)/shard_map/dot_general | solution.py:148
  322.7 29.1 %all_to_all.12 = f32[1,8,128,512]{3,2,0,1:T(8,128)S(1)} all-to-all(f32[1,8,128,512]{3,2,0,1:T(8,128)S(1)} %fusion.2), channel_id=1, replica_groups=mesh['col'=4,'grp'=8] {'grp'}, dimensions={1} | all-to-all | bytes 4194304 | tf_op jit(solution)/shard_map/all_to_all | solution.py:152
  351.8 3.5 copy.23
  (50 shorter events, 0.2 us)
Async XLA Ops:
  6.5 190.1 %all-reduce.2.cloned.1.call-start = ((), (), s32[]{:S(2)}) async-start(), calls=%async_computation.2 | async-start | bytes 8388608 | tf_op jit(solution)/shard_map/psum | solution.py:135
  15.8 1.6 copy-start.9
  17.4 2.2 copy-start.7
  19.5 0.7 copy-start.10
  20.2 20.0 %collective-permute-start = (f32[320,512]{1,0:T(8,128)S(1)}, f32[320,512]{1,0:T(8,128)}, u32[]{:S(2)}, u32[]{:S(2)}) collective-permute-start(f32[320,512]{1,0:T(8,128)S(1)} %pad_maximum_fusion), channel_id=1, source_target_pairs={{0,8},{8,16},{1,9},{9,17},{2,10},{10,18},{3,11},{11,19},{4,12},{12... | collective-permute-start | bytes 1966088 | tf_op jit(solution)/shard_map/ppermute | solution.py:107
  28.4 24.8 %collective-permute-start.4 = (f32[320,512]{1,0:T(8,128)}, f32[320,512]{1,0:T(8,128)}, u32[]{:S(2)}, u32[]{:S(2)}) collective-permute-start(f32[320,512]{1,0:T(8,128)} %bitcast.71), channel_id=1, source_target_pairs={{0,8},{8,16},{1,9},{9,17},{2,10},{10,18},{3,11},{11,19},{4,12},{12... | collective-permute-start | bytes 1966088 | tf_op jit(solution)/shard_map/ppermute | solution.py:107
  40.3 18.4 %collective-permute-start.1 = (f32[320,512]{1,0:T(8,128)}, f32[320,512]{1,0:T(8,128)}, u32[]{:S(2)}, u32[]{:S(2)}) collective-permute-start(f32[320,512]{1,0:T(8,128)} %collective-permute-done), channel_id=1, source_target_pairs={{8,16},{16,24},{9,17},{17,25},{10,18},{18,26},{11,19},{19,27},{12,... | collective-permute-start | bytes 1966088 | tf_op jit(solution)/shard_map/ppermute | solution.py:107
  41.8 22.4 %collective-permute-start.3 = (f32[320,512]{1,0:T(8,128)S(1)}, f32[320,512]{1,0:T(8,128)}, u32[]{:S(2)}, u32[]{:S(2)}) collective-permute-start(f32[320,512]{1,0:T(8,128)S(1)} %pad_maximum_fusion), channel_id=1, source_target_pairs={{8,0},{9,1},{10,2},{11,3},{12,4},{13,5},{14,6},{15,7}} | collective-permute-start | bytes 1966088 | tf_op jit(solution)/shard_map/ppermute | solution.py:101
  43.1 32.0 %collective-permute-start.7 = (f32[320,512]{1,0:T(8,128)}, f32[320,512]{1,0:T(8,128)}, u32[]{:S(2)}, u32[]{:S(2)}) collective-permute-start(f32[320,512]{1,0:T(8,128)} %bitcast.71), channel_id=1, source_target_pairs={{8,0},{9,1},{10,2},{11,3},{12,4},{13,5},{14,6},{15,7}} | collective-permute-start | bytes 1966088 | tf_op jit(solution)/shard_map/ppermute | solution.py:101
  53.3 7.7 %collective-permute-start.5 = (f32[320,512]{1,0:T(8,128)}, f32[320,512]{1,0:T(8,128)}, u32[]{:S(2)}, u32[]{:S(2)}) collective-permute-start(f32[320,512]{1,0:T(8,128)} %collective-permute-done.4), channel_id=1, source_target_pairs={{8,16},{16,24},{9,17},{17,25},{10,18},{18,26},{11,19},{19,27},{12,... | collective-permute-start | bytes 1966088 | tf_op jit(solution)/shard_map/ppermute | solution.py:107
  55.6 2.1 copy-start.15
  55.6 2.1 copy-start.16
  55.6 3.7 %copy-start.5 = (f32[512,1,1,512]{3,2,1,0:T(1,128)S(1)}, f32[512,1,1,512]{3,2,1,0:T(1,128)}, u32[]{:S(2)}) copy-start(f32[512,1,1,512]{3,2,1,0:T(1,128)} %get-tuple-element.8) | copy-start | bytes 3145732
  55.6 3.7 %copy-start.6 = (f32[512,1,1,512]{3,2,1,0:T(1,128)S(1)}, f32[512,1,1,512]{3,2,1,0:T(1,128)}, u32[]{:S(2)}) copy-start(f32[512,1,1,512]{3,2,1,0:T(1,128)} %get-tuple-element.9) | copy-start | bytes 3145732
  57.8 4.4 %copy-start.3 = (f32[512,1,1,512]{3,2,1,0:T(1,128)S(1)}, f32[512,1,1,512]{3,2,1,0:T(1,128)}, u32[]{:S(2)}) copy-start(f32[512,1,1,512]{3,2,1,0:T(1,128)} %get-tuple-element.6) | copy-start | bytes 3145732
  57.8 4.4 %copy-start.4 = (f32[512,1,1,512]{3,2,1,0:T(1,128)S(1)}, f32[512,1,1,512]{3,2,1,0:T(1,128)}, u32[]{:S(2)}) copy-start(f32[512,1,1,512]{3,2,1,0:T(1,128)} %get-tuple-element.7) | copy-start | bytes 3145732
  58.6 5.6 %collective-permute-start.2 = (f32[320,512]{1,0:T(8,128)}, f32[320,512]{1,0:T(8,128)S(1)}, u32[]{:S(2)}, u32[]{:S(2)}) collective-permute-start(f32[320,512]{1,0:T(8,128)} %collective-permute-done.1), channel_id=1, source_target_pairs={{16,24},{17,25},{18,26},{19,27},{20,28},{21,29},{22,30},{23,31}} | collective-permute-start | bytes 1966088 | tf_op jit(solution)/shard_map/ppermute | solution.py:107
  60.9 14.2 %collective-permute-start.6 = (f32[320,512]{1,0:T(8,128)}, f32[320,512]{1,0:T(8,128)S(1)}, u32[]{:S(2)}, u32[]{:S(2)}) collective-permute-start(f32[320,512]{1,0:T(8,128)} %collective-permute-done.5), channel_id=1, source_target_pairs={{16,24},{17,25},{18,26},{19,27},{20,28},{21,29},{22,30},{23,31}} | collective-permute-start | bytes 1966088 | tf_op jit(solution)/shard_map/ppermute | solution.py:107
  66.1 10.9 %copy-start.21 = (f32[320,512]{1,0:T(8,128)}, f32[320,512]{1,0:T(8,128)S(1)}, u32[]{:S(2)}) copy-start(f32[320,512]{1,0:T(8,128)S(1)} %get-tuple-element.22) | copy-start | bytes 1966084
  77.0 0.8 copy-start.23
  77.0 1.0 copy-start.25
  90.7 0.9 copy-start.13
  90.8 1.0 copy-start.14
  90.8 1.4 copy-start.2
  90.8 225.9 %reduce-scatter.2.cloned.1.call-start = ((), (), s32[]{:S(2)}) async-start(), calls=%async_computation.3 | async-start | bytes 18874368 | tf_op jit(solution)/shard_map/reduce_scatter | solution.py:145
  91.8 1.3 copy-start.8
  91.8 1.3 copy-start.11
  91.8 1.6 copy-start.22
  91.8 1.8 copy-start.24
  91.8 1.9 copy-start.26
  93.7 4.0 %copy-start.12 = (f32[512,1,1,512]{3,0,1,2:T(8,128)S(1)}, f32[512,1,1,512]{3,0,1,2:T(8,128)}, u32[]{:S(2)}) copy-start(f32[512,1,1,512]{3,0,1,2:T(8,128)} %copy.63) | copy-start | bytes 3145732
  97.8 4.0 %copy-start.19 = (f32[512,512]{1,0:T(8,128)S(1)}, f32[512,512]{1,0:T(8,128)}, u32[]{:S(2)}) copy-start(f32[512,512]{1,0:T(8,128)} %get-tuple-element.30) | copy-start | bytes 3145732
  97.8 4.0 %copy-start.28 = (f32[128,512]{1,0:T(8,128)S(1)}, f32[128,512]{1,0:T(8,128)}, u32[]{:S(2)}) copy-start(f32[128,512]{1,0:T(8,128)} %get-tuple-element.36) | copy-start | bytes 786436
  101.8 4.1 %copy-start.17 = (f32[512,512]{1,0:T(8,128)S(1)}, f32[512,512]{1,0:T(8,128)}, u32[]{:S(2)}) copy-start(f32[512,512]{1,0:T(8,128)} %get-tuple-element.29) | copy-start | bytes 3145732
  101.8 4.1 %copy-start.27 = (f32[128,512]{1,0:T(8,128)S(1)}, f32[128,512]{1,0:T(8,128)}, u32[]{:S(2)}) copy-start(f32[128,512]{1,0:T(8,128)} %get-tuple-element.35) | copy-start | bytes 786436
  105.9 4.1 %copy-start.20 = (f32[512,512]{1,0:T(8,128)S(1)}, f32[512,512]{1,0:T(8,128)}, u32[]{:S(2)}) copy-start(f32[512,512]{1,0:T(8,128)} %get-tuple-element.28) | copy-start | bytes 3145732
  105.9 4.1 %copy-start.30 = (f32[128,512]{1,0:T(8,128)S(1)}, f32[128,512]{1,0:T(8,128)}, u32[]{:S(2)}) copy-start(f32[128,512]{1,0:T(8,128)} %get-tuple-element.34) | copy-start | bytes 786436
  110.0 4.3 %copy-start.18 = (f32[512,512]{1,0:T(8,128)S(1)}, f32[512,512]{1,0:T(8,128)}, u32[]{:S(2)}) copy-start(f32[512,512]{1,0:T(8,128)} %get-tuple-element.27) | copy-start | bytes 3145732
  110.0 4.3 %copy-start.29 = (f32[128,512]{1,0:T(8,128)S(1)}, f32[128,512]{1,0:T(8,128)}, u32[]{:S(2)}) copy-start(f32[128,512]{1,0:T(8,128)} %get-tuple-element.33) | copy-start | bytes 786436
  196.6 2.2 copy-start.1
  267.6 2.0 copy-start
Sparse Core Ops, SparseCore 0:
  90.9 105.6 all-reduce.1
  200.6 116.1 reduce-scatter.1

commit v2 on v1

--- a/solution.py
+++ b/solution.py
@@ -1,3 +1,5 @@
+import functools
+
 import jax
 import jax.numpy as jnp
 from jax import lax
@@ -50,11 +52,85 @@
     return jnp.where(r >= c, done, 0.0)
 
 
+def upper_tiles(n):
+    count = n // TILE
+    return [(i, j) for i in range(count) for j in range(i, count)]
+
+
+def corner_sum_kernel(n, s_ref, out_ref, packed, slots, send_a, recv_a, send_b, recv_b):
+    me = lax.axis_index("grp")
+    rows = packed.shape[0] // n
+    mesh_id = pl.DeviceIdType.MESH
+    peers = [lax.rem(me + step, n) for step in range(1, n)]
+    barrier = pltpu.get_barrier_semaphore()
+    for peer in peers:
+        pl.semaphore_signal(barrier, inc=1, device_id={"grp": peer}, device_id_type=mesh_id)
+    for at, (i, j) in enumerate(upper_tiles(s_ref.shape[0])):
+        packed[at * TILE:(at + 1) * TILE, :] = s_ref[i * TILE:(i + 1) * TILE, j * TILE:(j + 1) * TILE]
+    pl.semaphore_wait(barrier, n - 1)
+    mine = pl.ds(pl.multiple_of(me * rows, 8), rows)
+    scatter = []
+    for at, peer in enumerate(peers):
+        copy = pltpu.make_async_remote_copy(
+            src_ref=packed.at[pl.ds(pl.multiple_of(peer * rows, 8), rows)],
+            dst_ref=slots.at[at],
+            send_sem=send_a.at[at], recv_sem=recv_a.at[at],
+            device_id={"grp": peer}, device_id_type=mesh_id,
+        )
+        copy.start()
+        scatter.append(copy)
+    total = packed[mine, :]
+    for at in range(n - 1):
+        scatter[at].wait_recv()
+        total = total + slots[at]
+    out_ref[mine, :] = total
+    gather = []
+    for at, peer in enumerate(peers):
+        copy = pltpu.make_async_remote_copy(
+            src_ref=out_ref.at[mine], dst_ref=out_ref.at[mine],
+            send_sem=send_b.at[at], recv_sem=recv_b.at[at],
+            device_id={"grp": peer}, device_id_type=mesh_id,
+        )
+        copy.start()
+        gather.append(copy)
+    for at, peer in enumerate(peers):
+        back = lax.rem(me + n - 1 - at, n)
+        pltpu.make_async_remote_copy(
+            src_ref=out_ref.at[mine],
+            dst_ref=out_ref.at[pl.ds(pl.multiple_of(back * rows, 8), rows)],
+            send_sem=send_b.at[at], recv_sem=recv_b.at[at],
+            device_id={"grp": peer}, device_id_type=mesh_id,
+        ).wait_recv()
+        scatter[at].wait_send()
+        gather[at].wait_send()
+
+
+def corner_sum(s, ngrp):
+    total = len(upper_tiles(s.shape[0])) * TILE
+    dma = pltpu.SemaphoreType.DMA((ngrp - 1,))
+    return pl.pallas_call(
+        functools.partial(corner_sum_kernel, ngrp),
+        out_shape=jax.ShapeDtypeStruct((total, TILE), jnp.float32),
+        in_specs=[pl.BlockSpec(memory_space=pltpu.VMEM)],
+        out_specs=pl.BlockSpec(memory_space=pltpu.VMEM),
+        scratch_shapes=[
+            pltpu.VMEM((total, TILE), jnp.float32),
+            pltpu.VMEM((ngrp - 1, total // ngrp, TILE), jnp.float32),
+            dma, dma, dma, dma,
+        ],
+        compiler_params=pltpu.CompilerParams(
+            collective_id=0, has_side_effects=True, vmem_limit_bytes=24 * 2**20
+        ),
+        cost_estimate=pl.CostEstimate(flops=40 * 10**9, bytes_accessed=8 * 2**20, transcendentals=0),
+    )(s)
+
+
 def inverse_factor_kernel(s_ref, m_ref):
-    n = s_ref.shape[0]
+    n = m_ref.shape[0]
     count = n // TILE
     highest = lax.Precision.HIGHEST
-    m_ref[...] = s_ref[...]
+    for at, (i, j) in enumerate(upper_tiles(n)):
+        m_ref[i * TILE:(i + 1) * TILE, j * TILE:(j + 1) * TILE] = s_ref[at * TILE:(at + 1) * TILE, :]
     r = lax.broadcasted_iota(jnp.int32, (TILE, TILE), 0)
     c = lax.broadcasted_iota(jnp.int32, (TILE, TILE), 1)
     eye = jnp.where(r == c, 1.0, 0.0).astype(jnp.float32)
@@ -84,8 +160,7 @@
         m_ref[here, :] = jnp.where(row >= col, m_ref[here, :], 0.0)
 
 
-def inverse_factor(s):
-    n = s.shape[0]
+def inverse_factor(s, n):
     return pl.pallas_call(
         inverse_factor_kernel,
         out_shape=jax.ShapeDtypeStruct((n, n), jnp.float32),
@@ -96,17 +171,22 @@
     )(s)
 
 
-def leading_panels(panel, ncol):
-    me = lax.axis_index("col")
+def chain(panel, ncol):
     back = lax.ppermute(panel, "col", [(1, 0)])
-    first = panel
-    second = jnp.where(me == 0, back, panel)
-    sent = panel
+    sent, steps = panel, []
     for t in range(ncol - 1):
         pairs = [(t, t + 1)] + ([(t + 1, t + 2)] if t + 2 < ncol else [])
         sent = lax.ppermute(sent, "col", pairs)
+        steps.append(sent)
+    return back, steps
+
+
+def chosen(panel, back, steps):
+    me = lax.axis_index("col")
+    first, second = panel, jnp.where(me == 0, back, panel)
+    for t, sent in enumerate(steps):
         first = jnp.where(me == t + 1, sent, first)
-        if t + 2 < ncol:
+        if t + 1 < len(steps):
             second = jnp.where(me == t + 2, sent, second)
     return first, second
 
@@ -117,33 +197,45 @@
         own_rows = factor_rows.shape[0]
         npanel = factor_rows.shape[1]
         width = factor_rows.shape[3]
-        panels = [
+        lead = jnp.concatenate([factor_rows[:, 0, 0, :], new_rows[:, 0, 0, :]], 0)
+        half = width // 2
+        lead, factor_rows, new_rows = lax.optimization_barrier((lead, factor_rows, new_rows))
+        panels = [lead] + [
             jnp.concatenate([factor_rows[:, p, 0, :], new_rows[:, p, 0, :]], 0)
-            for p in range(npanel)
+            for p in range(1, npanel)
         ]
-        total = panels[0].shape[0]
-        cut = total // 2
-        top = leading_panels(panels[0][:cut], ncol)
-        low = leading_panels(panels[0][cut:], ncol)
-        both = jnp.concatenate(
-            [jnp.concatenate(top, 1), jnp.concatenate(low, 1)], 0
-        )
         split = max(1, ngrp // npanel)
         piece = width // split
+        per = npanel * split // ngrp
         turned = (((0,), (0,)), ((), ()))
+        back_a, steps_a = chain(lead[:, :half], ncol)
+        back_b, steps_b = chain(lead[:, half:], ncol)
+        back_a, steps_a, back_b, early_b = lax.optimization_barrier(
+            (back_a, steps_a, back_b, steps_b[:-1])
+        )
+        first_a, second_a = chosen(lead[:, :half], back_a, steps_a)
+        first_b, second_b = chosen(lead[:, half:], back_b, early_b + steps_b[-1:])
+
+        def gram_rows(left):
+            return jnp.stack([
+                lax.dot_general(
+                    left, x[:, q * piece:(q + 1) * piece], turned,
+                    precision=high, preferred_element_type=jnp.float32,
+                )
+                for x in panels for q in range(split)
+            ], 0)
+
+        gram_a = gram_rows(jnp.concatenate([first_a, second_a], 1))
+        sum_a = lax.psum_scatter(gram_a, "grp", scatter_dimension=0, tiled=True)
+        both = jnp.concatenate([first_a, first_b, second_a, second_b], 1)
         corner = lax.dot_general(both, both, turned, precision=highest, preferred_element_type=jnp.float32)
-        corner = lax.psum(corner, "grp")
-        parts = [
-            lax.dot_general(
-                both, x[:, q * piece:(q + 1) * piece], turned,
-                precision=high, preferred_element_type=jnp.float32,
-            )
-            for x in panels for q in range(split)
-        ]
-        per = npanel * split // ngrp
-        gram = jnp.stack(parts, 0)
-        gram = lax.psum_scatter(gram, "grp", scatter_dimension=0, tiled=True)
-        inverse = inverse_factor(corner)
+        gram_b = gram_rows(jnp.concatenate([first_b, second_b], 1))
+        gram_b, corner = lax.optimization_barrier((gram_b, corner))
+        sum_b = lax.psum_scatter(gram_b, "grp", scatter_dimension=0, tiled=True)
+        inverse = inverse_factor(corner_sum(corner, ngrp), 2 * width)
+        gram = jnp.concatenate(
+            [sum_a[:, :half], sum_b[:, :half], sum_a[:, half:], sum_b[:, half:]], 1
+        )
         done = [
             jnp.dot(inverse, gram[p], precision=high, preferred_element_type=jnp.float32)
             for p in range(per)

time: 367 us -> 353 us (0.962)
  waiting for transfers between devices: 144 us -> 52.1 us
  Pallas kernels: 68.8 us -> 145 us
  matrix products: 51.2 us -> 57.9 us
  local copies, waits for them, and re-layouts: 34.3 us -> 30 us
    pallas_call x0 -> x1, Pallas kernels: none -> 76 us  [corner_sum(): pl.pallas_call(functools.partial(corner_sum_kernel, ngrp), out_shape=jax....]
    psum x1 -> x0, waiting for transfers between devices: 70.2 us -> none  [shards(): corner = lax.psum(corner, 'grp')]
    reduce_scatter x1 -> x2, waiting for transfers between devices: 47.2 us -> 32.2 us  [the longest x1 32.1 us: shards(): sum_b = lax.psum_scatter(gram_b, 'grp', scatter_dimension=0, tiled=True)]
    dot_general x8 -> x16, matrix products: 32.5 us -> 40.6 us  [gram_rows(): lax.dot_general(left, x[:, q * piece:(q + 1) * piece], turned, precision=...]
    ppermute x8, waiting for transfers between devices: 26.7 us -> 19.9 us  [the longest x6 19.9 us: chain(): sent = lax.ppermute(sent, 'col', pairs)]
    unnamed x70 -> x76, local copies, waits for them, and re-layouts: 16.2 us -> 10 us
  transfers between devices with their start and end apart: 10 -> 10, of which waited for: 6 -> 3; matrix products, arithmetic and copies ran while one was open for 12% -> 13% of each run, Pallas kernels for 19% -> 42%
where the time goes in v2:
time: 353 us; the launch traced here: 348 us
  Pallas kernels  145 us (41%)
  matrix products  57.9 us (16%)
  waiting for transfers between devices  52.1 us (15%)
  local copies, waits for them, and re-layouts  30 us (8%)
  blocking collectives  29.1 us (8%)
  starting transfers between devices  17.4 us (5%)
  between operations  14 us (4%)
    pallas_call x1, Pallas kernels, corner_sum(): pl.pallas_call(functools.partial(corner_sum_kernel, ngrp), out_shape=jax....  76 us
    pallas_call x1, Pallas kernels, inverse_factor(): pl.pallas_call(inverse_factor_kernel, out_shape=jax.ShapeDtypeStruct((n,...  68.5 us
    dot_general x16, matrix products, gram_rows(): lax.dot_general(left, x[:, q * piece:(q + 1) * piece], turned, precision=...  40.6 us
    reduce_scatter x1, waiting for transfers between devices, shards(): sum_b = lax.psum_scatter(gram_b, 'grp', scatter_dimension=0, tiled=True)  32.1 us
    all_to_all x1, blocking collectives, shards(): lax.all_to_all(result, 'grp', split_axis=1, concat_axis=0, tiled=True)  29.1 us
    ppermute x6, waiting for transfers between devices, chain(): sent = lax.ppermute(sent, 'col', pairs)  19.9 us
    ppermute x6, starting transfers between devices, chain(): sent = lax.ppermute(sent, 'col', pairs)  14.4 us
    dot_general x1, matrix products, shards(): lax.dot_general(both, both, turned, precision=highest, preferred_element_...  11.9 us
  transfers between devices with their start and end apart: 10, of which 3 were waited for; matrix products, arithmetic and copies ran while one was open for 13% of the time, Pallas kernels for 42%

profile of v2, /device:TPU:0, one launch (start us, length us, event | category | flops | bytes accessed | tf_op | source)
XLA Modules:
  0.0 347.6 jit_solution(9770762567793260845)
XLA Ops:
  6.5 1.2 slice-done
  7.8 0.1 copy.41
  7.9 0.1 pad_maximum_fusion
  8.0 0.0 copy-start.2
  8.0 1.2 fusion.49
  9.2 0.3 copy-done.2
  9.5 6.1 %collective-permute-start.4 = (f32[640,256]{1,0:T(8,128)}, f32[640,256]{1,0:T(8,128)}, u32[]{:S(2)}, u32[]{:S(2)}) collective-permute-start(f32[640,256]{1,0:T(8,128)} %get-tuple-element.50), channel_id=1, source_target_pairs={{0,8},{8,16},{1,9},{9,17},{2,10},{10,18},{3,11},{11,19},{4,12},{12... | collective-permute-start | bytes 1966088 | tf_op jit(solution)/shard_map/ppermute | solution.py:179
  15.5 3.5 %collective-permute-start = (f32[640,256]{1,0:T(8,128)}, f32[640,256]{1,0:T(8,128)}, u32[]{:S(2)}, u32[]{:S(2)}) collective-permute-start(f32[640,256]{1,0:T(8,128)} %get-tuple-element.49), channel_id=1, source_target_pairs={{0,8},{8,16},{1,9},{9,17},{2,10},{10,18},{3,11},{11,19},{4,12},{12... | collective-permute-start | bytes 1966088 | tf_op jit(solution)/shard_map/ppermute | solution.py:179
  19.0 1.3 collective-permute-start.3
  20.3 1.3 collective-permute-start.7
  21.6 8.5 %collective-permute-done.4 = f32[640,256]{1,0:T(8,128)} collective-permute-done((f32[640,256]{1,0:T(8,128)}, f32[640,256]{1,0:T(8,128)}, u32[]{:S(2)}, u32[]{:S(2)}) %collective-permute-start.4) | collective-permute-done | bytes 655392 | tf_op jit(solution)/shard_map/ppermute | solution.py:179
  30.1 1.5 collective-permute-start.5
  31.6 11.4 %collective-permute-done = f32[640,256]{1,0:T(8,128)} collective-permute-done((f32[640,256]{1,0:T(8,128)}, f32[640,256]{1,0:T(8,128)}, u32[]{:S(2)}, u32[]{:S(2)}) %collective-permute-start) | collective-permute-done | bytes 655392 | tf_op jit(solution)/shard_map/ppermute | solution.py:179
  43.0 1.5 collective-permute-start.1
  44.5 8.6 %fusion.48 = (f32[512,1,1,512]{3,2,1,0:T(1,128)S(1)}, f32[512,1,1,512]{3,2,1,0:T(1,128)S(1)}, f32[512,1,1,512]{3,2,1,0:T(1,128)S(1)}, f32[512,1,1,512]{3,2,1,0:T...) fusion(f32[512,8,1,512]{3,2,1,0:T(1,128)S(1)} %copy-done.18), kind=kLoop, calls=%fused_computation.95 | loop fusion | bytes 14680064 | tf_op jit(solution)/shard_map/slice | solution.py:204
  53.1 2.8 copy.13
  55.9 0.1 copy.40
  56.0 0.2 slice_bitcast_fusion
  56.2 1.7 copy-done.21
  58.0 0.5 copy-done.22
  58.4 0.2 copy_bitcast_fusion.5
  58.6 0.0 collective-permute-done.5
  58.6 0.8 collective-permute-start.6
  59.5 0.0 collective-permute-done.1
  59.5 1.0 collective-permute-start.2
  60.5 0.2 copy-done.20
  60.7 0.2 copy_bitcast_fusion.3
  60.9 0.0 copy-start.3
  60.9 0.2 copy_bitcast_fusion.1
  61.1 0.0 collective-permute-done.3
  61.2 0.0 collective-permute-done.7
  61.2 0.0 collective-permute-done.6
  61.2 2.1 copy-done.3
  63.2 2.5 select_select_fusion.1
  65.7 2.4 fusion.23
  68.1 2.4 fusion.22
  70.6 2.4 fusion.21
  73.0 2.5 fusion.20
  75.5 2.4 fusion.19
  77.9 2.4 fusion.18
  80.3 2.4 fusion.17
  82.7 2.4 fusion.16
  85.1 0.0 reduce-scatter.3.cloned.1.call-update
  85.2 0.4 reduce-scatter.5.cloned.1.call-start
  85.6 3.9 %fusion.31 = f32[8,512,512]{2,1,0:T(8,128)} fusion(f32[640,512]{1,0:T(8,128)} %copy-done.2, f32[640,256]{1,0:T(8,128)S(1)} %get-tuple-element.47, f32[640,256]{1,0:T(8,128)S(1)} %get-tuple-element.48), kind=kOutput, calls=%fused_computation.48 | convolution fusion | flops 1006960640 | bytes 3670016 | tf_op jit(solution)/shard_map/dot_general | solution.py:221
  89.5 2.5 fusion.30
  92.0 2.5 fusion.29
  94.5 2.5 fusion.28
  97.0 2.5 fusion.27
  99.5 2.5 fusion.26
  101.9 2.5 fusion.25
  104.4 2.5 fusion.24
  106.9 11.9 %fusion.s_ref = f32[1024,1024]{1,0:T(8,128)} fusion(f32[640,256]{1,0:T(8,128)S(1)} %get-tuple-element.47, f32[640,256]{1,0:T(8,128)S(1)} %get-tuple-element.37, f32[640,256]{1,0:T(8,128)S(1)} %get-tuple-element.48, f32[640,256]{1,0:T(8,128)S(1)} %get-tuple-element.36), kind=kOutput, calls=%fused_computation | convolution fusion | flops 8055029760 | bytes 6815744 | tf_op jit(solution)/shard_map/dot_general | solution.py:231
  118.9 0.0 reduce-scatter.5.cloned.1.call-update
  118.9 2.4 copy-done.1
  121.3 76.0 %shard_map.28.s_ref = f32[4608,128]{1,0:T(8,128)S(1)} custom-call(f32[1024,1024]{1,0:T(8,128)S(1)} %copy-done.1), custom_call_target="tpu_custom_call" | custom-call | flops 40000000000 | bytes 8388608 | tf_op jit(solution)/shard_map/pallas_call | solution.py:111
  197.4 68.5 %shard_map.29 = f32[1024,1024]{1,0:T(8,128)S(1)} custom-call(f32[4608,128]{1,0:T(8,128)S(1)} %shard_map.28.s_ref), custom_call_target="tpu_custom_call" | custom-call | flops 60000002048 | bytes 8388608 | tf_op jit(solution)/shard_map/pallas_call | solution.py:164
  265.9 2.0 copy-done
  267.9 1.3 fusion.50
  269.1 32.1 %reduce-scatter.5.cloned.1.call-done = f32[1,512,512]{2,1,0:T(8,128)} async-done(((f32[8,512,512]{2,1,0:T(8,128)}), f32[1,512,512]{2,1,0:T(8,128)}) %reduce-scatter.5.cloned.1.call-update) | async-done | bytes 1048592 | tf_op jit(solution)/shard_map/reduce_scatter | solution.py:234
  301.3 1.3 fusion.51
  302.5 5.4 %fusion.15 = f32[1,8,128,512]{3,2,0,1:T(8,128)S(1)} fusion(f32[8,128,1024]{2,1,0:T(8,128)} %bitcast.116, f32[1,256,512]{2,1,0:T(8,128)S(1)} %get-tuple-element.54, f32[1,256,512]{2,1,0:T(8,128)S(1)} %get-tuple-element.52, f32[1,256,512]{2,1,0:T(8,128)S(1)} %get-tuple-element.53, f32[1,256,512]{2,1,0:T(8,128)S(1)} %get-tuple-element.51), kind=kOutput, calls=%fused_computation.16 | convolution fusion | flops 3222798336 | bytes 8388608 | tf_op jit(solution)/shard_map/dot_general | solution.py:240
  307.9 29.1 %all_to_all.12 = f32[1,8,128,512]{3,2,0,1:T(8,128)S(1)} all-to-all(f32[1,8,128,512]{3,2,0,1:T(8,128)S(1)} %fusion.15), channel_id=1, replica_groups=mesh['col'=4,'grp'=8] {'grp'}, dimensions={1} | all-to-all | bytes 4194304 | tf_op jit(solution)/shard_map/all_to_all | solution.py:244
  337.0 3.5 %copy.21 = f32[128,8,1,512]{3,2,1,0:T(1,128)} copy(f32[128,8,1,512]{3,0,1,2:T(8,128)S(1)} %bitcast.119) | data formatting | bytes 4194304 | tf_op jit(solution)/shard_map/transpose | solution.py:246
  (68 shorter events, 0.2 us)
Async XLA Ops:
  6.5 1.2 slice-start
  6.5 261.3 %reduce-scatter.3.cloned.1.call-start = ((), (), s32[]{:S(2)}) async-start(), calls=%async_computation.3 | async-start | bytes 9437184 | tf_op jit(solution)/shard_map/reduce_scatter | solution.py:229
  6.5 1.3 slice-start.1
  7.8 36.7 %copy-start.18 = (f32[512,8,1,512]{3,2,1,0:T(1,128)S(1)}, f32[512,8,1,512]{3,2,1,0:T(1,128)}, u32[]{:S(2)}) copy-start(f32[512,8,1,512]{3,2,1,0:T(1,128)} %param.3) | copy-start | bytes 25165828
  8.0 1.5 copy-start.2
  9.5 20.6 %collective-permute-start.4 = (f32[640,256]{1,0:T(8,128)}, f32[640,256]{1,0:T(8,128)}, u32[]{:S(2)}, u32[]{:S(2)}) collective-permute-start(f32[640,256]{1,0:T(8,128)} %get-tuple-element.50), channel_id=1, source_target_pairs={{0,8},{8,16},{1,9},{9,17},{2,10},{10,18},{3,11},{11,19},{4,12},{12... | collective-permute-start | bytes 1966088 | tf_op jit(solution)/shard_map/ppermute | solution.py:179
  15.5 27.5 %collective-permute-start = (f32[640,256]{1,0:T(8,128)}, f32[640,256]{1,0:T(8,128)}, u32[]{:S(2)}, u32[]{:S(2)}) collective-permute-start(f32[640,256]{1,0:T(8,128)} %get-tuple-element.49), channel_id=1, source_target_pairs={{0,8},{8,16},{1,9},{9,17},{2,10},{10,18},{3,11},{11,19},{4,12},{12... | collective-permute-start | bytes 1966088 | tf_op jit(solution)/shard_map/ppermute | solution.py:179
  19.0 42.1 %collective-permute-start.3 = (f32[640,256]{1,0:T(8,128)}, f32[640,256]{1,0:T(8,128)}, u32[]{:S(2)}, u32[]{:S(2)}) collective-permute-start(f32[640,256]{1,0:T(8,128)} %get-tuple-element.50), channel_id=1, source_target_pairs={{8,0},{9,1},{10,2},{11,3},{12,4},{13,5},{14,6},{15,7}} | collective-permute-start | bytes 1966088 | tf_op jit(solution)/shard_map/ppermute | solution.py:175
  20.3 40.9 %collective-permute-start.7 = (f32[640,256]{1,0:T(8,128)}, f32[640,256]{1,0:T(8,128)}, u32[]{:S(2)}, u32[]{:S(2)}) collective-permute-start(f32[640,256]{1,0:T(8,128)} %get-tuple-element.49), channel_id=1, source_target_pairs={{8,0},{9,1},{10,2},{11,3},{12,4},{13,5},{14,6},{15,7}} | collective-permute-start | bytes 1966088 | tf_op jit(solution)/shard_map/ppermute | solution.py:175
  30.1 28.5 %collective-permute-start.5 = (f32[640,256]{1,0:T(8,128)}, f32[640,256]{1,0:T(8,128)}, u32[]{:S(2)}, u32[]{:S(2)}) collective-permute-start(f32[640,256]{1,0:T(8,128)} %collective-permute-done.4), channel_id=1, source_target_pairs={{8,16},{16,24},{9,17},{17,25},{10,18},{18,26},{11,19},{19,27},{12,... | collective-permute-start | bytes 1966088 | tf_op jit(solution)/shard_map/ppermute | solution.py:179
  43.0 16.5 %collective-permute-start.1 = (f32[640,256]{1,0:T(8,128)}, f32[640,256]{1,0:T(8,128)}, u32[]{:S(2)}, u32[]{:S(2)}) collective-permute-start(f32[640,256]{1,0:T(8,128)} %collective-permute-done), channel_id=1, source_target_pairs={{8,16},{16,24},{9,17},{17,25},{10,18},{18,26},{11,19},{19,27},{12,... | collective-permute-start | bytes 1966088 | tf_op jit(solution)/shard_map/ppermute | solution.py:179
  55.9 26.8 %copy-start.4 = (f32[512,1,1,512]{3,0,1,2:T(8,128)}, f32[512,1,1,512]{3,0,1,2:T(8,128)S(1)}, u32[]{:S(2)}) copy-start(f32[512,1,1,512]{3,0,1,2:T(8,128)S(1)} %copy.40) | copy-start | bytes 3145732
  56.0 2.0 copy-start.21
  56.0 2.5 copy-start.22
  56.2 12.0 %copy-start.33 = (f32[128,512]{1,0:T(8,128)}, f32[128,512]{1,0:T(8,128)S(1)}, u32[]{:S(2)}) copy-start(f32[128,512]{1,0:T(8,128)S(1)} %get-tuple-element.46) | copy-start | bytes 786436
  56.2 14.4 %copy-start.31 = (f32[128,512]{1,0:T(8,128)}, f32[128,512]{1,0:T(8,128)S(1)}, u32[]{:S(2)}) copy-start(f32[128,512]{1,0:T(8,128)S(1)} %get-tuple-element.45) | copy-start | bytes 786436
  56.2 16.8 %copy-start.29 = (f32[128,512]{1,0:T(8,128)}, f32[128,512]{1,0:T(8,128)S(1)}, u32[]{:S(2)}) copy-start(f32[128,512]{1,0:T(8,128)S(1)} %get-tuple-element.44) | copy-start | bytes 786436
  56.2 19.2 %copy-start.27 = (f32[128,512]{1,0:T(8,128)}, f32[128,512]{1,0:T(8,128)S(1)}, u32[]{:S(2)}) copy-start(f32[128,512]{1,0:T(8,128)S(1)} %get-tuple-element.43) | copy-start | bytes 786436
  56.2 21.7 %copy-start.25 = (f32[128,512]{1,0:T(8,128)}, f32[128,512]{1,0:T(8,128)S(1)}, u32[]{:S(2)}) copy-start(f32[128,512]{1,0:T(8,128)S(1)} %get-tuple-element.42) | copy-start | bytes 786436
  56.2 24.1 %copy-start.23 = (f32[128,512]{1,0:T(8,128)}, f32[128,512]{1,0:T(8,128)S(1)}, u32[]{:S(2)}) copy-start(f32[128,512]{1,0:T(8,128)S(1)} %get-tuple-element.41) | copy-start | bytes 786436
  58.4 2.1 copy-start.19
  58.4 2.3 copy-start.20
  58.6 9.5 %copy-start.8 = (f32[512,512]{1,0:T(8,128)}, f32[512,512]{1,0:T(8,128)S(1)}, u32[]{:S(2)}) copy-start(f32[512,512]{1,0:T(8,128)S(1)} %get-tuple-element.60) | copy-start | bytes 3145732
  58.6 11.9 %copy-start.6 = (f32[512,512]{1,0:T(8,128)}, f32[512,512]{1,0:T(8,128)S(1)}, u32[]{:S(2)}) copy-start(f32[512,512]{1,0:T(8,128)S(1)} %get-tuple-element.59) | copy-start | bytes 3145732
  58.6 2.5 collective-permute-start.6
  59.5 1.7 collective-permute-start.2
  60.9 12.1 %copy-start.16 = (f32[512,512]{1,0:T(8,128)}, f32[512,512]{1,0:T(8,128)S(1)}, u32[]{:S(2)}) copy-start(f32[512,512]{1,0:T(8,128)S(1)} %get-tuple-element.58) | copy-start | bytes 3145732
  60.9 14.5 %copy-start.12 = (f32[512,512]{1,0:T(8,128)}, f32[512,512]{1,0:T(8,128)S(1)}, u32[]{:S(2)}) copy-start(f32[512,512]{1,0:T(8,128)S(1)} %get-tuple-element.57) | copy-start | bytes 3145732
  60.9 2.3 copy-start.3
  61.1 16.8 %copy-start.14 = (f32[512,512]{1,0:T(8,128)}, f32[512,512]{1,0:T(8,128)S(1)}, u32[]{:S(2)}) copy-start(f32[512,512]{1,0:T(8,128)S(1)} %get-tuple-element.56) | copy-start | bytes 3145732
  61.1 19.1 %copy-start.10 = (f32[512,512]{1,0:T(8,128)}, f32[512,512]{1,0:T(8,128)S(1)}, u32[]{:S(2)}) copy-start(f32[512,512]{1,0:T(8,128)S(1)} %get-tuple-element.55) | copy-start | bytes 3145732
  85.2 216.1 %reduce-scatter.5.cloned.1.call-start = ((), (), s32[]{:S(2)}) async-start(), calls=%async_computation.4 | async-start | bytes 9437184 | tf_op jit(solution)/shard_map/reduce_scatter | solution.py:234
  85.6 3.9 %copy-start.9 = (f32[512,512]{1,0:T(8,128)S(1)}, f32[512,512]{1,0:T(8,128)}, u32[]{:S(2)}) copy-start(f32[512,512]{1,0:T(8,128)} %copy-done.8) | copy-start | bytes 3145732
  85.6 3.9 %copy-start.34 = (f32[128,512]{1,0:T(8,128)S(1)}, f32[128,512]{1,0:T(8,128)}, u32[]{:S(2)}) copy-start(f32[128,512]{1,0:T(8,128)} %copy-done.33) | copy-start | bytes 786436
  89.5 2.5 copy-start.7
  89.5 2.5 copy-start.32
  92.0 2.5 copy-start.17
  92.0 2.5 copy-start.30
  94.5 2.5 copy-start.13
  94.5 2.5 copy-start.28
  97.0 2.5 copy-start.15
  97.0 2.5 copy-start.26
  99.4 2.5 copy-start.11
  99.5 2.5 copy-start.24
  101.9 2.5 copy-start.5
  118.9 2.5 copy-start.1
  265.9 2.0 copy-start
Sparse Core Ops, SparseCore 0:
  85.3 137.4 reduce-scatter.2
  226.6 74.5 reduce-scatter.4

commit v3 on v1

--- a/solution.py
+++ b/solution.py
@@ -51,10 +51,13 @@
 
 
 def inverse_factor_kernel(s_ref, m_ref):
-    n = s_ref.shape[0]
+    n = m_ref.shape[0]
     count = n // TILE
     highest = lax.Precision.HIGHEST
-    m_ref[...] = s_ref[...]
+    band, at = s_ref.shape[0], 0
+    for top in range(0, n, band):
+        m_ref[top:top + band, top:] = s_ref[:, at:at + n - top]
+        at += n - top
     r = lax.broadcasted_iota(jnp.int32, (TILE, TILE), 0)
     c = lax.broadcasted_iota(jnp.int32, (TILE, TILE), 1)
     eye = jnp.where(r == c, 1.0, 0.0).astype(jnp.float32)
@@ -84,8 +87,7 @@
         m_ref[here, :] = jnp.where(row >= col, m_ref[here, :], 0.0)
 
 
-def inverse_factor(s):
-    n = s.shape[0]
+def inverse_factor(s, n):
     return pl.pallas_call(
         inverse_factor_kernel,
         out_shape=jax.ShapeDtypeStruct((n, n), jnp.float32),
@@ -96,17 +98,22 @@
     )(s)
 
 
-def leading_panels(panel, ncol):
-    me = lax.axis_index("col")
+def chain(panel, ncol):
     back = lax.ppermute(panel, "col", [(1, 0)])
-    first = panel
-    second = jnp.where(me == 0, back, panel)
-    sent = panel
+    sent, steps = panel, []
     for t in range(ncol - 1):
         pairs = [(t, t + 1)] + ([(t + 1, t + 2)] if t + 2 < ncol else [])
         sent = lax.ppermute(sent, "col", pairs)
+        steps.append(sent)
+    return back, steps
+
+
+def chosen(panel, back, steps):
+    me = lax.axis_index("col")
+    first, second = panel, jnp.where(me == 0, back, panel)
+    for t, sent in enumerate(steps):
         first = jnp.where(me == t + 1, sent, first)
-        if t + 2 < ncol:
+        if t + 1 < len(steps):
             second = jnp.where(me == t + 2, sent, second)
     return first, second
 
@@ -117,33 +124,46 @@
         own_rows = factor_rows.shape[0]
         npanel = factor_rows.shape[1]
         width = factor_rows.shape[3]
-        panels = [
+        lead = jnp.concatenate([factor_rows[:, 0, 0, :], new_rows[:, 0, 0, :]], 0)
+        half = width // 2
+        lead, factor_rows, new_rows = lax.optimization_barrier((lead, factor_rows, new_rows))
+        panels = [lead] + [
             jnp.concatenate([factor_rows[:, p, 0, :], new_rows[:, p, 0, :]], 0)
-            for p in range(npanel)
+            for p in range(1, npanel)
         ]
-        total = panels[0].shape[0]
-        cut = total // 2
-        top = leading_panels(panels[0][:cut], ncol)
-        low = leading_panels(panels[0][cut:], ncol)
-        both = jnp.concatenate(
-            [jnp.concatenate(top, 1), jnp.concatenate(low, 1)], 0
-        )
         split = max(1, ngrp // npanel)
         piece = width // split
+        per = npanel * split // ngrp
         turned = (((0,), (0,)), ((), ()))
-        corner = lax.dot_general(both, both, turned, precision=highest, preferred_element_type=jnp.float32)
-        corner = lax.psum(corner, "grp")
-        parts = [
+        back_a, steps_a = chain(lead[:, :half], ncol)
+        back_b, steps_b = chain(lead[:, half:], ncol)
+        back_a, steps_a, back_b, steps_b = lax.optimization_barrier(
+            (back_a, steps_a, back_b, steps_b)
+        )
+        first_a, second_a = chosen(lead[:, :half], back_a, steps_a)
+        first_b, second_b = chosen(lead[:, half:], back_b, steps_b)
+
+        def gram_rows(left):
+            return jnp.stack([
+                lax.dot_general(
+                    left, x[:, q * piece:(q + 1) * piece], turned,
+                    precision=high, preferred_element_type=jnp.float32,
+                )
+                for x in panels for q in range(split)
+            ], 0)
+
+        both = jnp.concatenate([first_a, first_b, second_a, second_b], 1)
+        packed = jnp.concatenate([
             lax.dot_general(
-                both, x[:, q * piece:(q + 1) * piece], turned,
-                precision=high, preferred_element_type=jnp.float32,
+                both[:, at:at + half], both[:, at:], turned,
+                precision=highest, preferred_element_type=jnp.float32,
             )
-            for x in panels for q in range(split)
-        ]
-        per = npanel * split // ngrp
-        gram = jnp.stack(parts, 0)
-        gram = lax.psum_scatter(gram, "grp", scatter_dimension=0, tiled=True)
-        inverse = inverse_factor(corner)
+            for at in range(0, 2 * width, half)
+        ], 1)
+        packed, both = lax.optimization_barrier((packed, both))
+        packed = lax.psum(packed, "grp")
+        gram = lax.psum_scatter(gram_rows(both), "grp", scatter_dimension=0, tiled=True)
+        inverse = inverse_factor(packed, 2 * width)
         done = [
             jnp.dot(inverse, gram[p], precision=high, preferred_element_type=jnp.float32)
             for p in range(per)

time: 367 us -> 344 us (0.937)
  waiting for transfers between devices: 144 us -> 128 us
  local copies, waits for them, and re-layouts: 34.3 us -> 29.1 us
    psum x1, waiting for transfers between devices: 70.2 us -> 61.1 us  [shards(): packed = lax.psum(packed, 'grp')]
    ppermute x8, waiting for transfers between devices: 26.7 us -> 19.9 us  [the longest x6 19.9 us: chain(): sent = lax.ppermute(sent, 'col', pairs)]
    unnamed x70 -> x52, local copies, waits for them, and re-layouts: 16.2 us -> 12 us
    dot_general x9 -> x12, matrix products: 45.3 us -> 43 us  [the longest x8 35.4 us: gram_rows(): lax.dot_general(left, x[:, q * piece:(q + 1) * piece], turned, precision=...]
  transfers between devices with their start and end apart: 10 -> 10, of which waited for: 6 -> 4; matrix products, arithmetic and copies ran while one was open for 12% -> 14% of each run, Pallas kernels for 19% -> 20%
where the time goes in v3:
time: 344 us; the launch traced here: 339 us
  waiting for transfers between devices  128 us (37%)
  Pallas kernels  68.6 us (20%)
  matrix products  48.9 us (14%)
  local copies, waits for them, and re-layouts  29.1 us (8%)
  blocking collectives  29.1 us (8%)
  starting transfers between devices  17.1 us (5%)
  between operations  13.8 us (4%)
  other arithmetic  4.71 us (1%)
    pallas_call x1, Pallas kernels, inverse_factor(): pl.pallas_call(inverse_factor_kernel, out_shape=jax.ShapeDtypeStruct((n,...  68.6 us
    psum x1, waiting for transfers between devices, shards(): packed = lax.psum(packed, 'grp')  61.1 us
    reduce_scatter x1, waiting for transfers between devices, shards(): lax.psum_scatter(gram_rows(both), 'grp', scatter_dimension=0, tiled=True)  46.9 us
    dot_general x8, matrix products, gram_rows(): lax.dot_general(left, x[:, q * piece:(q + 1) * piece], turned, precision=...  35.4 us
    all_to_all x1, blocking collectives, shards(): lax.all_to_all(result, 'grp', split_axis=1, concat_axis=0, tiled=True)  29.1 us
    ppermute x6, waiting for transfers between devices, chain(): sent = lax.ppermute(sent, 'col', pairs)  19.9 us
    ppermute x6, starting transfers between devices, chain(): sent = lax.ppermute(sent, 'col', pairs)  14.2 us
    unnamed x52, local copies, waits for them, and re-layouts  12 us
  transfers between devices with their start and end apart: 10, of which 4 were waited for; matrix products, arithmetic and copies ran while one was open for 14% of the time, Pallas kernels for 20%

profile of v3, /device:TPU:0, one launch (start us, length us, event | category | flops | bytes accessed | tf_op | source)
XLA Modules:
  0.0 339.3 jit_solution(15240265573561437350)
XLA Ops:
  6.5 0.0 all-reduce.2.cloned.1.call-start
  6.5 1.2 slice-done
  7.8 0.1 copy.44
  7.8 0.0 slice-done.1
  7.9 0.1 pad_maximum_fusion.2
  8.0 0.0 copy-start.2
  8.0 1.2 fusion.47
  9.1 6.1 %collective-permute-start.1 = (f32[640,256]{1,0:T(8,128)}, f32[640,256]{1,0:T(8,128)}, u32[]{:S(2)}, u32[]{:S(2)}) collective-permute-start(f32[640,256]{1,0:T(8,128)} %get-tuple-element.52), channel_id=1, source_target_pairs={{0,8},{8,16},{1,9},{9,17},{2,10},{10,18},{3,11},{11,19},{4,12},{12... | collective-permute-start | bytes 1966088 | tf_op jit(solution)/shard_map/ppermute | solution.py:106
  15.2 3.5 %collective-permute-start.5 = (f32[640,256]{1,0:T(8,128)}, f32[640,256]{1,0:T(8,128)}, u32[]{:S(2)}, u32[]{:S(2)}) collective-permute-start(f32[640,256]{1,0:T(8,128)} %get-tuple-element.51), channel_id=1, source_target_pairs={{0,8},{8,16},{1,9},{9,17},{2,10},{10,18},{3,11},{11,19},{4,12},{12... | collective-permute-start | bytes 1966088 | tf_op jit(solution)/shard_map/ppermute | solution.py:106
  18.7 1.3 collective-permute-start
  19.9 1.3 collective-permute-start.4
  21.2 8.5 %collective-permute-done.1 = f32[640,256]{1,0:T(8,128)} collective-permute-done((f32[640,256]{1,0:T(8,128)}, f32[640,256]{1,0:T(8,128)}, u32[]{:S(2)}, u32[]{:S(2)}) %collective-permute-start.1) | collective-permute-done | bytes 655392 | tf_op jit(solution)/shard_map/ppermute | solution.py:106
  29.8 1.5 collective-permute-start.2
  31.3 11.4 %collective-permute-done.5 = f32[640,256]{1,0:T(8,128)} collective-permute-done((f32[640,256]{1,0:T(8,128)}, f32[640,256]{1,0:T(8,128)}, u32[]{:S(2)}, u32[]{:S(2)}) %collective-permute-start.5) | collective-permute-done | bytes 655392 | tf_op jit(solution)/shard_map/ppermute | solution.py:106
  42.7 1.5 collective-permute-start.6
  44.2 0.0 copy-done.3
  44.2 8.7 %fusion.46 = (f32[512,1,1,512]{3,2,1,0:T(1,128)S(1)}, f32[512,1,1,512]{3,2,1,0:T(1,128)}, f32[512,1,1,512]{3,2,1,0:T(1,128)}, f32[512,1,1,512]{3,2,1,0:T(1,128)}...) fusion(f32[512,8,1,512]{3,2,1,0:T(1,128)S(1)} %copy-done.3), kind=kLoop, calls=%fused_computation.75 | loop fusion | bytes 14680064 | tf_op jit(solution)/shard_map/slice | solution.py:131
  52.9 1.2 copy.43
  54.1 0.8 copy-done.15
  54.9 1.2 copy.15
  56.1 0.0 copy-start.7
  56.1 1.3 slice_bitcast_fusion
  57.4 0.6 copy-done.7
  57.9 0.3 copy-done.8
  58.3 1.6 copy_bitcast_fusion.4
  59.9 0.0 collective-permute-done.2
  59.9 0.8 collective-permute-start.3
  60.7 0.0 collective-permute-done.6
  60.7 0.9 collective-permute-start.7
  61.6 1.5 copy_bitcast_fusion.2
  63.1 0.0 copy-done.4
  63.1 1.5 copy_bitcast_fusion
  64.6 0.0 collective-permute-done
  64.6 0.0 collective-permute-done.4
  64.6 0.0 collective-permute-done.3
  64.6 0.0 collective-permute-done.7
  64.7 2.5 select_select_fusion.3
  67.2 0.4 pad_maximum_fusion
  67.6 2.8 fusion.45
  70.4 2.2 fusion.2
  72.5 1.4 fusion.11
  74.0 1.2 fusion.48
  75.2 1.7 pad_maximum_fusion.1
  77.0 5.3 %bitcast_dynamic-update-slice_fusion.7 = f32[8,1024,512]{2,1,0:T(8,128)} fusion(f32[640,1024]{1,0:T(8,128)S(1)} %pad_maximum_fusion, f32[640,512]{1,0:T(8,128)} %copy-done.2), kind=kOutput, calls=%fused_computation.11 | convolution fusion | flops 2013265920 | bytes 6029312 | tf_op jit(solution)/shard_map/dot_general | solution.py:148
  82.3 0.0 all-reduce.2.cloned.1.call-update
  82.3 0.3 reduce-scatter.2.cloned.1.call-start
  82.6 0.7 copy-done.22
  83.2 5.3 %bitcast_dynamic-update-slice_fusion.6 = f32[8,1024,512]{2,1,0:T(8,128)} fusion(f32[8,1024,512]{2,1,0:T(8,128)} %bitcast_dynamic-update-slice_fusion.7, f32[640,1024]{1,0:T(8,128)S(1)} %pad_maximum_fusion, f32[512,512]{1,0:T(8,128)} %bitcast.83, f32[128,512]{1,0:T(8,128)S(1)} %copy-done.22), kind=kOutput, calls=%fused_computation.10 | convolution fusion | flops 2013593600 | bytes 6029312 | tf_op jit(solution)/shard_map/dot_general | solution.py:148
  88.6 4.1 %bitcast_dynamic-update-slice_fusion.5 = f32[8,1024,512]{2,1,0:T(8,128)} fusion(f32[8,1024,512]{2,1,0:T(8,128)} %bitcast_dynamic-update-slice_fusion.6, f32[640,1024]{1,0:T(8,128)S(1)} %pad_maximum_fusion, f32[512,512]{1,0:T(8,128)S(1)} %copy-done.10, f32[128,512]{1,0:T(8,128)S(1)} %copy-done.21), kind=kOutput, calls=%fused_computation.9 | convolution fusion | flops 2013593600 | bytes 6029312 | tf_op jit(solution)/shard_map/dot_general | solution.py:148
  92.7 4.1 %bitcast_dynamic-update-slice_fusion.4 = f32[8,1024,512]{2,1,0:T(8,128)} fusion(f32[8,1024,512]{2,1,0:T(8,128)} %bitcast_dynamic-update-slice_fusion.5, f32[640,1024]{1,0:T(8,128)S(1)} %pad_maximum_fusion, f32[512,512]{1,0:T(8,128)S(1)} %copy-done.9, f32[128,512]{1,0:T(8,128)S(1)} %copy-done.20), kind=kOutput, calls=%fused_computation.8 | convolution fusion | flops 2013593600 | bytes 6029312 | tf_op jit(solution)/shard_map/dot_general | solution.py:148
  96.8 4.0 %bitcast_dynamic-update-slice_fusion.3 = f32[8,1024,512]{2,1,0:T(8,128)} fusion(f32[8,1024,512]{2,1,0:T(8,128)} %bitcast_dynamic-update-slice_fusion.4, f32[640,1024]{1,0:T(8,128)S(1)} %pad_maximum_fusion, f32[512,512]{1,0:T(8,128)S(1)} %copy-done.14, f32[128,512]{1,0:T(8,128)S(1)} %copy-done.19), kind=kOutput, calls=%fused_computation.7 | convolution fusion | flops 2013593600 | bytes 6029312 | tf_op jit(solution)/shard_map/dot_general | solution.py:148
  100.8 4.5 %bitcast_dynamic-update-slice_fusion.2 = f32[8,1024,512]{2,1,0:T(8,128)} fusion(f32[8,1024,512]{2,1,0:T(8,128)} %bitcast_dynamic-update-slice_fusion.3, f32[640,1024]{1,0:T(8,128)S(1)} %pad_maximum_fusion, f32[512,512]{1,0:T(8,128)S(1)} %copy-done.12, f32[128,512]{1,0:T(8,128)S(1)} %copy-done.18), kind=kOutput, calls=%fused_computation.6 | convolution fusion | flops 2013593600 | bytes 6029312 | tf_op jit(solution)/shard_map/dot_general | solution.py:148
  105.3 4.0 %bitcast_dynamic-update-slice_fusion.1 = f32[8,1024,512]{2,1,0:T(8,128)} fusion(f32[8,1024,512]{2,1,0:T(8,128)} %bitcast_dynamic-update-slice_fusion.2, f32[640,1024]{1,0:T(8,128)S(1)} %pad_maximum_fusion, f32[512,512]{1,0:T(8,128)S(1)} %copy-done.13, f32[128,512]{1,0:T(8,128)S(1)} %copy-done.17), kind=kOutput, calls=%fused_computation.5 | convolution fusion | flops 2013593600 | bytes 6029312 | tf_op jit(solution)/shard_map/dot_general | solution.py:148
  109.3 0.0 copy-done.11
  109.4 4.0 %bitcast_dynamic-update-slice_fusion = f32[8,1024,512]{2,1,0:T(8,128)} fusion(f32[8,1024,512]{2,1,0:T(8,128)} %bitcast_dynamic-update-slice_fusion.1, f32[640,1024]{1,0:T(8,128)S(1)} %pad_maximum_fusion, f32[512,512]{1,0:T(8,128)S(1)} %copy-done.11, f32[128,512]{1,0:T(8,128)S(1)} %copy-done.16), kind=kOutput, calls=%fused_computation.4 | convolution fusion | flops 2013593600 | bytes 6029312 | tf_op jit(solution)/shard_map/dot_general | solution.py:148
  113.3 0.0 reduce-scatter.2.cloned.1.call-update
  113.4 61.1 %all-reduce.2.cloned.1.call-done.s_ref = f32[256,2560]{1,0:T(8,128)} async-done(((f32[256,2560]{1,0:T(8,128)}), f32[256,2560]{1,0:T(8,128)}) %all-reduce.2.cloned.1.call-update) | async-done | bytes 2621456 | tf_op jit(solution)/shard_map/psum | solution.py:164
  174.4 1.7 copy-done.1
  176.2 68.6 %shard_map.28 = f32[1024,1024]{1,0:T(8,128)S(1)} custom-call(f32[256,2560]{1,0:T(8,128)S(1)} %copy-done.1), custom_call_target="tpu_custom_call" | custom-call | flops 60000002048 | bytes 8388608 | tf_op jit(solution)/shard_map/pallas_call | solution.py:91
  244.8 2.0 copy-done
  246.8 46.9 %reduce-scatter.2.cloned.1.call-done = f32[1,1024,512]{2,1,0:T(8,128)} async-done(((f32[8,1024,512]{2,1,0:T(8,128)}), f32[1,1024,512]{2,1,0:T(8,128)}) %reduce-scatter.2.cloned.1.call-update) | async-done | bytes 2097168 | tf_op jit(solution)/shard_map/reduce_scatter | solution.py:165
  293.7 5.9 %fusion.8 = f32[1,8,128,512]{3,2,0,1:T(8,128)S(1)} fusion(f32[8,128,1024]{2,1,0:T(8,128)} %bitcast.80, f32[1,1024,512]{2,1,0:T(8,128)} %reduce-scatter.2.cloned.1.call-done), kind=kOutput, calls=%fused_computation.18 | convolution fusion | flops 3221225472 | bytes 8388608 | tf_op jit(solution)/shard_map/dot_general | solution.py:168
  299.6 29.1 %all_to_all.12 = f32[1,8,128,512]{3,2,0,1:T(8,128)S(1)} all-to-all(f32[1,8,128,512]{3,2,0,1:T(8,128)S(1)} %fusion.8), channel_id=1, replica_groups=mesh['col'=4,'grp'=8] {'grp'}, dimensions={1} | all-to-all | bytes 4194304 | tf_op jit(solution)/shard_map/all_to_all | solution.py:172
  328.8 3.5 %copy.23 = f32[128,8,1,512]{3,2,1,0:T(1,128)} copy(f32[128,8,1,512]{3,0,1,2:T(8,128)S(1)} %bitcast.81) | data formatting | bytes 4194304 | tf_op jit(solution)/shard_map/transpose | solution.py:174
  (38 shorter events, 0.1 us)
Async XLA Ops:
  6.5 1.2 slice-start
  6.5 1.3 slice-start.1
  6.5 167.9 %all-reduce.2.cloned.1.call-start = ((), (), s32[]{:S(2)}) async-start(), calls=%async_computation.2 | async-start | bytes 5242880 | tf_op jit(solution)/shard_map/psum | solution.py:164
  7.8 36.4 %copy-start.3 = (f32[512,8,1,512]{3,2,1,0:T(1,128)S(1)}, f32[512,8,1,512]{3,2,1,0:T(1,128)}, u32[]{:S(2)}) copy-start(f32[512,8,1,512]{3,2,1,0:T(1,128)} %param.3) | copy-start | bytes 25165828
  8.0 56.7 %copy-start.2 = (f32[640,512]{1,0:T(8,128)}, f32[640,512]{1,0:T(8,128)S(1)}, u32[]{:S(2)}) copy-start(f32[640,512]{1,0:T(8,128)S(1)} %pad_maximum_fusion.2) | copy-start | bytes 3932164
  9.1 20.6 %collective-permute-start.1 = (f32[640,256]{1,0:T(8,128)}, f32[640,256]{1,0:T(8,128)}, u32[]{:S(2)}, u32[]{:S(2)}) collective-permute-start(f32[640,256]{1,0:T(8,128)} %get-tuple-element.52), channel_id=1, source_target_pairs={{0,8},{8,16},{1,9},{9,17},{2,10},{10,18},{3,11},{11,19},{4,12},{12... | collective-permute-start | bytes 1966088 | tf_op jit(solution)/shard_map/ppermute | solution.py:106
  15.2 27.5 %collective-permute-start.5 = (f32[640,256]{1,0:T(8,128)}, f32[640,256]{1,0:T(8,128)}, u32[]{:S(2)}, u32[]{:S(2)}) collective-permute-start(f32[640,256]{1,0:T(8,128)} %get-tuple-element.51), channel_id=1, source_target_pairs={{0,8},{8,16},{1,9},{9,17},{2,10},{10,18},{3,11},{11,19},{4,12},{12... | collective-permute-start | bytes 1966088 | tf_op jit(solution)/shard_map/ppermute | solution.py:106
  18.7 46.0 %collective-permute-start = (f32[640,256]{1,0:T(8,128)}, f32[640,256]{1,0:T(8,128)}, u32[]{:S(2)}, u32[]{:S(2)}) collective-permute-start(f32[640,256]{1,0:T(8,128)} %get-tuple-element.52), channel_id=1, source_target_pairs={{8,0},{9,1},{10,2},{11,3},{12,4},{13,5},{14,6},{15,7}} | collective-permute-start | bytes 1966088 | tf_op jit(solution)/shard_map/ppermute | solution.py:102
  19.9 44.7 %collective-permute-start.4 = (f32[640,256]{1,0:T(8,128)}, f32[640,256]{1,0:T(8,128)}, u32[]{:S(2)}, u32[]{:S(2)}) collective-permute-start(f32[640,256]{1,0:T(8,128)} %get-tuple-element.51), channel_id=1, source_target_pairs={{8,0},{9,1},{10,2},{11,3},{12,4},{13,5},{14,6},{15,7}} | collective-permute-start | bytes 1966088 | tf_op jit(solution)/shard_map/ppermute | solution.py:102
  29.8 30.1 %collective-permute-start.2 = (f32[640,256]{1,0:T(8,128)}, f32[640,256]{1,0:T(8,128)}, u32[]{:S(2)}, u32[]{:S(2)}) collective-permute-start(f32[640,256]{1,0:T(8,128)} %collective-permute-done.1), channel_id=1, source_target_pairs={{8,16},{16,24},{9,17},{17,25},{10,18},{18,26},{11,19},{19,27},{12,... | collective-permute-start | bytes 1966088 | tf_op jit(solution)/shard_map/ppermute | solution.py:106
  42.7 18.0 %collective-permute-start.6 = (f32[640,256]{1,0:T(8,128)}, f32[640,256]{1,0:T(8,128)}, u32[]{:S(2)}, u32[]{:S(2)}) collective-permute-start(f32[640,256]{1,0:T(8,128)} %collective-permute-done.5), channel_id=1, source_target_pairs={{8,16},{16,24},{9,17},{17,25},{10,18},{18,26},{11,19},{19,27},{12,... | collective-permute-start | bytes 1966088 | tf_op jit(solution)/shard_map/ppermute | solution.py:106
  52.9 2.0 copy-start.15
  56.1 1.9 copy-start.7
  56.1 2.2 copy-start.8
  57.4 4.2 %copy-start.5 = (f32[512,1,1,512]{3,2,1,0:T(1,128)S(1)}, f32[512,1,1,512]{3,2,1,0:T(1,128)}, u32[]{:S(2)}) copy-start(f32[512,1,1,512]{3,2,1,0:T(1,128)} %get-tuple-element.33) | copy-start | bytes 3145732
  57.4 4.2 %copy-start.6 = (f32[512,1,1,512]{3,2,1,0:T(1,128)S(1)}, f32[512,1,1,512]{3,2,1,0:T(1,128)}, u32[]{:S(2)}) copy-start(f32[512,1,1,512]{3,2,1,0:T(1,128)} %get-tuple-element.34) | copy-start | bytes 3145732
  59.8 3.3 copy-start.4
  59.9 4.8 %collective-permute-start.3 = (f32[640,256]{1,0:T(8,128)}, f32[640,256]{1,0:T(8,128)S(1)}, u32[]{:S(2)}, u32[]{:S(2)}) collective-permute-start(f32[640,256]{1,0:T(8,128)} %collective-permute-done.2), channel_id=1, source_target_pairs={{16,24},{17,25},{18,26},{19,27},{20,28},{21,29},{22,30},{23,31}} | collective-permute-start | bytes 1966088 | tf_op jit(solution)/shard_map/ppermute | solution.py:106
  60.7 3.9 %collective-permute-start.7 = (f32[640,256]{1,0:T(8,128)}, f32[640,256]{1,0:T(8,128)S(1)}, u32[]{:S(2)}, u32[]{:S(2)}) collective-permute-start(f32[640,256]{1,0:T(8,128)} %collective-permute-done.6), channel_id=1, source_target_pairs={{16,24},{17,25},{18,26},{19,27},{20,28},{21,29},{22,30},{23,31}} | collective-permute-start | bytes 1966088 | tf_op jit(solution)/shard_map/ppermute | solution.py:106
  82.3 0.9 copy-start.22
  82.3 211.4 %reduce-scatter.2.cloned.1.call-start = ((), (), s32[]{:S(2)}) async-start(), calls=%async_computation.3 | async-start | bytes 18874368 | tf_op jit(solution)/shard_map/reduce_scatter | solution.py:165
  83.2 5.3 %copy-start.10 = (f32[512,512]{1,0:T(8,128)S(1)}, f32[512,512]{1,0:T(8,128)}, u32[]{:S(2)}) copy-start(f32[512,512]{1,0:T(8,128)} %get-tuple-element.58) | copy-start | bytes 3145732
  83.2 5.3 %copy-start.21 = (f32[128,512]{1,0:T(8,128)S(1)}, f32[128,512]{1,0:T(8,128)}, u32[]{:S(2)}) copy-start(f32[128,512]{1,0:T(8,128)} %get-tuple-element.47) | copy-start | bytes 786436
  88.6 4.1 %copy-start.9 = (f32[512,512]{1,0:T(8,128)S(1)}, f32[512,512]{1,0:T(8,128)}, u32[]{:S(2)}) copy-start(f32[512,512]{1,0:T(8,128)} %get-tuple-element.57) | copy-start | bytes 3145732
  88.6 4.1 %copy-start.20 = (f32[128,512]{1,0:T(8,128)S(1)}, f32[128,512]{1,0:T(8,128)}, u32[]{:S(2)}) copy-start(f32[128,512]{1,0:T(8,128)} %get-tuple-element.46) | copy-start | bytes 786436
  92.7 4.1 %copy-start.14 = (f32[512,512]{1,0:T(8,128)S(1)}, f32[512,512]{1,0:T(8,128)}, u32[]{:S(2)}) copy-start(f32[512,512]{1,0:T(8,128)} %get-tuple-element.56) | copy-start | bytes 3145732
  92.7 4.1 %copy-start.19 = (f32[128,512]{1,0:T(8,128)S(1)}, f32[128,512]{1,0:T(8,128)}, u32[]{:S(2)}) copy-start(f32[128,512]{1,0:T(8,128)} %get-tuple-element.45) | copy-start | bytes 786436
  96.8 4.1 %copy-start.12 = (f32[512,512]{1,0:T(8,128)S(1)}, f32[512,512]{1,0:T(8,128)}, u32[]{:S(2)}) copy-start(f32[512,512]{1,0:T(8,128)} %get-tuple-element.55) | copy-start | bytes 3145732
  96.8 4.1 %copy-start.18 = (f32[128,512]{1,0:T(8,128)S(1)}, f32[128,512]{1,0:T(8,128)}, u32[]{:S(2)}) copy-start(f32[128,512]{1,0:T(8,128)} %get-tuple-element.44) | copy-start | bytes 786436
  100.8 4.5 %copy-start.13 = (f32[512,512]{1,0:T(8,128)S(1)}, f32[512,512]{1,0:T(8,128)}, u32[]{:S(2)}) copy-start(f32[512,512]{1,0:T(8,128)} %get-tuple-element.54) | copy-start | bytes 3145732
  100.8 4.5 %copy-start.17 = (f32[128,512]{1,0:T(8,128)S(1)}, f32[128,512]{1,0:T(8,128)}, u32[]{:S(2)}) copy-start(f32[128,512]{1,0:T(8,128)} %get-tuple-element.43) | copy-start | bytes 786436
  105.3 4.0 %copy-start.11 = (f32[512,512]{1,0:T(8,128)S(1)}, f32[512,512]{1,0:T(8,128)}, u32[]{:S(2)}) copy-start(f32[512,512]{1,0:T(8,128)} %get-tuple-element.53) | copy-start | bytes 3145732
  105.3 4.0 %copy-start.16 = (f32[128,512]{1,0:T(8,128)S(1)}, f32[128,512]{1,0:T(8,128)}, u32[]{:S(2)}) copy-start(f32[128,512]{1,0:T(8,128)} %get-tuple-element.42) | copy-start | bytes 786436
  174.4 1.7 copy-start.1
  244.8 2.0 copy-start
Sparse Core Ops, SparseCore 0:
  82.4 91.9 all-reduce.1
  178.0 115.6 reduce-scatter.1
